TPU v7x, 128 devices: a whole 4x4x4 slice. The times are simulated.
128 devices in a mesh: frame: 32 (over x, y, core), row: 4 (over z).
Axes of the slice: x: 4, y: 4, z: 4, core: 2. Of those that a mesh axis runs over, the one named last changes fastest.
Arguments:
- hidden_in: bfloat16 [64, 1024, 1024], P('frame', 'row'), may hold values from -6 to 6
- query_weight: bfloat16 [1024, 1024], replicated, as said below
- kv_weight: bfloat16 [1024, 2048], replicated, may hold values from -0.1875 to 0.1875
- out_weight: bfloat16 [1024, 1024], replicated, may hold values from -0.1875 to 0.1875
- proj_in: bfloat16 [1024, 256], replicated, may hold values from -0.1875 to 0.1875
- proj_attn: bfloat16 [1024, 256], replicated, may hold values from -0.1875 to 0.1875
- camera_table: bfloat16 [6, 256], replicated, may hold values from -6 to 6
- camera_id: int32 [64], replicated, may hold values from 0 to 5
- t_query: bfloat16 [256, 256], replicated
- t_kv: bfloat16 [256, 512], replicated, may hold values from -0.375 to 0.375
- t_out: bfloat16 [256, 256], replicated, may hold values from -0.375 to 0.375
- depth_read: float32 [256], replicated, may hold values from -0.375 to 0.375
- lidar_pixel: int32 [64, 512], P('frame'), may hold values from 0 to 1023
- lidar_depth: float32 [64, 512], P('frame'), may hold values from 1 to 80
- lidar_valid: int32 [64, 512], P('frame'), may hold values from 0 to 1
Outputs:
- depth_map: float32 [64, 1024], P('frame', 'row')
- point_error: float32 [64, 512], P('frame')
- loss: float32 [], replicated
Inputs may be any that keep to these rules, and one draw needn't show every extreme that they name: `query_weight`: query projection weights.
All inputs are finite; a program needn't handle non-finite values.
Results may differ from a plain program's by a relative error of at most 0.0085.
Values may be sent and summed in bfloat16 or wider, within the bound.
A program may use at most 128 MiB of HBM per device.

v0:
```python
import math

import jax
import jax.numpy as jnp
from jax import lax
from jax.sharding import PartitionSpec as P

HEADS = 16
T_HEADS = 8
CAMERAS = 6


def normalize(values):
    mean = jnp.mean(values, axis=-1, keepdims=True)
    centred = values - mean
    var = jnp.mean(centred * centred, axis=-1, keepdims=True)
    return centred * lax.rsqrt(var + 1e-06)


def body(
    hidden_in,
    query_weight,
    kv_weight,
    out_weight,
    proj_in,
    proj_attn,
    camera_table,
    camera_id,
    t_query,
    t_kv,
    t_out,
    depth_read,
    lidar_pixel,
    lidar_depth,
    lidar_valid,
):
    frames_dev, tok_dev, width = hidden_in.shape
    head_dim = width // HEADS
    head_width = proj_in.shape[1]
    t_dim = head_width // T_HEADS
    flat = hidden_in.reshape(frames_dev * tok_dev, width)
    normed = normalize(flat.astype(jnp.float32)).astype(jnp.bfloat16)
    query = jnp.dot(normed, query_weight, preferred_element_type=jnp.float32).astype(jnp.bfloat16)
    query = query.reshape(frames_dev, tok_dev, HEADS, head_dim)
    keyval = jnp.dot(normed, kv_weight, preferred_element_type=jnp.float32).astype(jnp.bfloat16)
    keyval = keyval.reshape(frames_dev, tok_dev, 2 * width)
    piece = lax.all_gather(keyval, "row", axis=1, tiled=True)
    best = jnp.full((frames_dev, HEADS, tok_dev), -1e30, jnp.float32)
    count = piece.shape[1]
    keys = piece[:, :, :width].reshape(frames_dev, count, HEADS, head_dim)
    values = piece[:, :, width:].reshape(frames_dev, count, HEADS, head_dim)
    scores = jnp.einsum(
        "fqhd,fkhd->fhqk", query, keys, preferred_element_type=jnp.float32
    ) / math.sqrt(head_dim)
    newbest = jnp.maximum(best, jnp.max(scores, axis=-1))
    probs = jnp.exp(scores - newbest[..., None])
    total = jnp.sum(probs, axis=-1)
    accum = jnp.einsum(
        "fhqk,fkhd->fhqd", probs.astype(jnp.bfloat16), values, preferred_element_type=jnp.float32
    )
    best, total, accum = (newbest, total, accum)
    attn = (accum / total[..., None]).astype(jnp.bfloat16)
    attn = jnp.transpose(attn, (0, 2, 1, 3)).reshape(frames_dev * tok_dev, width)
    mixed = flat.astype(jnp.float32) + jnp.dot(attn, out_weight, preferred_element_type=jnp.float32)
    after = normalize(mixed).astype(jnp.bfloat16)
    parts = lax.axis_size("frame")
    block = tok_dev // parts
    onehot = (camera_id[:, None] == jnp.arange(CAMERAS, dtype=jnp.int32)[None, :]).astype(
        jnp.float32
    )
    cam_rows = jnp.dot(onehot, camera_table.astype(jnp.float32), precision=lax.Precision.HIGHEST)
    first_frame = lax.axis_index("frame") * frames_dev
    local_cam = lax.dynamic_slice_in_dim(cam_rows, first_frame, frames_dev, 0)
    feat = jnp.dot(normed, proj_in, preferred_element_type=jnp.float32)
    feat = feat + jnp.dot(after, proj_attn, preferred_element_type=jnp.float32)
    feat = (feat.reshape(frames_dev, tok_dev, head_width) + local_cam[:, None, :]).astype(
        jnp.bfloat16
    )
    feat = feat.reshape(frames_dev, parts, block, head_width)
    temporal_feat = lax.all_to_all(feat, "frame", split_axis=1, concat_axis=0, tiled=True)[:, 0]
    frames_all, count, _ = temporal_feat.shape
    normed_t = (
        normalize(temporal_feat.astype(jnp.float32)).astype(jnp.bfloat16).reshape(-1, head_width)
    )
    tq = jnp.dot(normed_t, t_query, preferred_element_type=jnp.float32).astype(jnp.bfloat16)
    tkv = jnp.dot(normed_t, t_kv, preferred_element_type=jnp.float32).astype(jnp.bfloat16)
    tq = tq.reshape(frames_all, count, T_HEADS, t_dim)
    tkv = tkv.reshape(frames_all, count, 2 * head_width)
    t_keys = tkv[:, :, :head_width].reshape(frames_all, count, T_HEADS, t_dim)
    t_values = tkv[:, :, head_width:].reshape(frames_all, count, T_HEADS, t_dim)
    scores = jnp.einsum(
        "tphd,sphd->phts", tq, t_keys, preferred_element_type=jnp.float32
    ) / math.sqrt(t_dim)
    probs = jnp.exp(scores - jnp.max(scores, axis=-1, keepdims=True))
    sums = jnp.sum(probs, axis=-1)
    numer = jnp.einsum(
        "phts,sphd->tphd", probs.astype(jnp.bfloat16), t_values, preferred_element_type=jnp.float32
    )
    tattn = (
        (numer / jnp.transpose(sums, (2, 0, 1))[..., None])
        .astype(jnp.bfloat16)
        .reshape(-1, head_width)
    )
    latent = temporal_feat.astype(jnp.float32).reshape(-1, head_width) + jnp.dot(
        tattn, t_out, preferred_element_type=jnp.float32
    )
    depth_vals = 0.1 + jax.nn.softplus(jnp.sum(latent * depth_read, axis=-1))
    depth_block = depth_vals.reshape(frames_all, count)[:, None, :]
    depth_local = lax.all_to_all(
        depth_block, "frame", split_axis=0, concat_axis=1, tiled=True
    ).reshape(frames_dev, tok_dev)
    row_start = lax.axis_index("row") * tok_dev
    local_index = lidar_pixel - row_start
    inside = (local_index >= 0) & (local_index < tok_dev)
    safe_index = jnp.clip(local_index, 0, tok_dev - 1)
    predicted = jnp.take_along_axis(depth_local, safe_index, axis=1)
    valid = lidar_valid.astype(jnp.float32)
    partial_error = jnp.where(inside, valid * (jnp.log(predicted) - jnp.log(lidar_depth)), 0.0)
    point_error = lax.psum(partial_error, "row")
    abs_total = lax.psum(jnp.sum(jnp.abs(point_error)), "frame")
    point_count = frames_dev * parts * lidar_valid.shape[1]
    loss = abs_total / float(point_count)
    return (depth_local, point_error, loss)


def solution(mesh):
    return jax.shard_map(
        body,
        mesh=mesh,
        in_specs=(
            P("frame", "row", None),
            P(),
            P(),
            P(),
            P(),
            P(),
            P(),
            P(),
            P(),
            P(),
            P(),
            P(),
            P("frame", None),
            P("frame", None),
            P("frame", None),
        ),
        out_specs=(P("frame", "row"), P("frame", None), P()),
        check_vma=False,
    )
```

profile of v0, /device:TPU:1, one launch (start us, length us, event | category | flops | bytes accessed | tf_op | source)
XLA Modules:
  0.0 308.4 jit_solution(16052133814003050161)
XLA Ops:
  7.2 1.6 convert_reduce_fusion
  8.9 1.6 fusion.10
  10.5 0.3 fusion.12
  10.9 6.3 %convolution_convert_fusion = bf16[512,2048]{1,0:T(8,128)(2,1)} fusion(bf16[512,1024]{1,0:T(8,128)(2,1)S(1)} %fusion.12, bf16[1024,2048]{1,0:T(8,128)(2,1)} %param.17), kind=kOutput, calls=%fused_computation.8 | convolution fusion | flops 2148532224 | bytes 7340032 | tf_op jit(solution)/shard_map/dot_general | solution.py:45
  17.2 4.1 %convolution_convert_fusion.1 = bf16[512,1024]{1,0:T(8,128)(2,1)} fusion(bf16[512,1024]{1,0:T(8,128)(2,1)} %copy-done.3, bf16[1024,1024]{1,0:T(8,128)(2,1)} %param.16), kind=kOutput, calls=%fused_computation.27 | convolution fusion | flops 1074266112 | bytes 4194304 | tf_op jit(solution)/shard_map/dot_general | solution.py:43
  21.4 4.1 %reshape.234 = bf16[2,256,16,64]{3,2,1,0:T(8,128)(2,1)} reshape(bf16[512,1024]{1,0:T(8,128)(2,1)} %convolution_convert_fusion.1) | data formatting | bytes 2097152 | tf_op jit(solution)/shard_map/reshape | solution.py:44
  25.4 0.2 fusion.32
  25.7 2.6 fusion.45
  28.3 75.6 %all-gather.2.cloned.1.call-done = bf16[2,1024,2048]{2,1,0:T(8,128)(2,1)} async-done(((bf16[2,256,2048]{2,1,0:T(8,128)(2,1)}), bf16[2,1024,2048]{2,1,0:T(8,128)(2,1)}) %all-gather.2.cloned.1.call-update) | async-done | bytes 8388624 | tf_op jit(solution)/shard_map/all_gather | solution.py:47
  103.9 5.9 %fusion.42 = (bf16[2,1024,1024]{2,1,0:T(8,128)(2,1)}, bf16[2,1024,1024]{2,1,0:T(8,128)(2,1)}) fusion(bf16[2,1024,2048]{2,1,0:T(8,128)(2,1)} %all-gather.2.cloned.1.call-done), kind=kLoop, calls=%fused_computation.77 | loop fusion | bytes 16777216 | tf_op jit(solution)/shard_map/slice | solution.py:50
  109.8 6.2 %copy.69 = bf16[2,1024,1024]{1,2,0:T(8,128)(2,1)} copy(bf16[2,1024,1024]{2,1,0:T(8,128)(2,1)} %get-tuple-element.4) | data formatting | bytes 8388608 | tf_op jit(solution)/shard_map/slice | solution.py:51
  116.0 6.2 %copy.67 = bf16[2,1024,1024]{1,2,0:T(8,128)(2,1)} copy(bf16[2,1024,1024]{2,1,0:T(8,128)(2,1)} %get-tuple-element.3) | data formatting | bytes 8388608 | tf_op jit(solution)/shard_map/slice | solution.py:50
  122.2 15.6 %multiply_reduce_fusion = (f32[2,16,256]{2,1,0:T(8,128)S(1)}, f32[2,16,256,1024]{3,2,1,0:T(8,128)}) fusion(bf16[2,1024,16,64]{1,3,2,0:T(8,128)(2,1)} %bitcast.91, bf16[2,256,16,64]{3,2,1,0:T(8,128)(2,1)} %reshape.234), kind=kOutput, calls=%fused_computation.2 | convolution fusion | flops 1090510848 | bytes 38830080 | tf_op jit(solution)/shard_map/fqhd,fkhd->fhqk/dot_general | solution.py:52
  137.9 14.2 %fusion = f32[2,16,256]{2,1,0:T(8,128)S(1)} fusion(f32[2,16,256,1024]{3,2,1,0:T(8,128)} %get-tuple-element.10, f32[2,16,256]{2,1,0:T(8,128)S(1)} %broadcast_maximum_fusion), kind=kLoop, calls=%fused_computation.3 | loop fusion | flops 25157632 | bytes 33619968 | tf_op jit(solution)/shard_map/reduce_sum | solution.py:57
  152.1 16.0 %fusion.6 = bf16[2,256,16,64]{1,3,2,0:T(8,128)(2,1)} fusion(bf16[2,1024,16,64]{1,3,2,0:T(8,128)(2,1)} %bitcast.93, f32[2,16,256,1024]{3,2,1,0:T(8,128)} %get-tuple-element.10, f32[2,16,256]{2,1,0:T(8,128)S(1)} %broadcast_maximum_fusion, f32[2,256,16]{1,2,0:T(8,128)S(1)} %bitcast.102), kind=kOutput, calls=%fused_computation.10 | convolution fusion | flops 1099956224 | bytes 38862848 | tf_op jit(solution)/shard_map/fhqk,fkhd->fhqd/dot_general | solution.py:58
  168.1 2.3 copy.70
  170.4 0.2 copy.90
  170.7 1.4 fusion.44
  172.1 0.3 multiply_reduce_fusion.1
  172.5 0.7 copy-done.4
  173.1 0.2 copy-done.6
  173.3 0.5 convolution_add_fusion
  173.8 0.7 fusion.31
  174.5 7.9 %all-to-all-start = ((bf16[2,32,8,256]{3,2,0,1:T(8,128)(2,1)}), bf16[2,32,8,256]{3,2,0,1:T(8,128)(2,1)S(1)}, u32[]{:S(2)}, u32[]{:S(2)}) async-start(bf16[2,32,8,256]{3,2,0,1:T(8,128)(2,1)} %fusion.31), calls=%async_computation | async-start | bytes 524288 | tf_op jit(solution)/shard_map/all_to_all | solution.py:80
  182.4 9.0 %all-to-all-done = bf16[2,32,8,256]{3,2,0,1:T(8,128)(2,1)S(1)} async-done(((bf16[2,32,8,256]{3,2,0,1:T(8,128)(2,1)}), bf16[2,32,8,256]{3,2,0,1:T(8,128)(2,1)S(1)}, u32[]{:S(2)}, u32[]{:S(2)}) %all-to-all-start) | async-done | bytes 262176 | tf_op jit(solution)/shard_map/all_to_all | solution.py:80
  191.5 1.0 copy.77
  192.5 0.2 bitcast_reduce_fusion
  192.7 0.1 div.67
  192.8 0.3 fusion.30
  193.2 0.2 multiply_convert_fusion.2
  193.4 0.3 fusion.19
  193.7 1.1 copy.72
  194.8 1.1 copy.73
  195.9 0.2 convolution_convert_fusion.3
  196.1 0.4 reshape.214
  196.6 2.4 multiply_reduce_fusion.2
  199.0 0.6 fusion.13
  199.6 1.3 fusion.18
  200.9 2.6 copy.76
  203.5 0.7 reshape.216
  204.3 1.3 fusion.21
  205.8 0.7 copy.83
  206.5 3.7 %all-to-all-start.1 = ((f32[64,1,8]{2,1,0:T(1,128)}), f32[64,1,8]{2,1,0:T(1,128)S(1)}, u32[]{:S(2)}, u32[]{:S(2)}) async-start(f32[64,1,8]{2,1,0:T(1,128)} %copy.83), calls=%async_computation.1 | async-start | bytes 65536 | tf_op jit(solution)/shard_map/all_to_all | solution.py:109
  210.2 7.3 %all-to-all-done.1 = f32[64,1,8]{2,1,0:T(1,128)S(1)} async-done(((f32[64,1,8]{2,1,0:T(1,128)}), f32[64,1,8]{2,1,0:T(1,128)S(1)}, u32[]{:S(2)}, u32[]{:S(2)}) %all-to-all-start.1) | async-done | bytes 2080 | tf_op jit(solution)/shard_map/all_to_all | solution.py:109
  217.7 9.1 %gather_fusion = f32[1024]{0:T(1024)S(1)} fusion(f32[2,256]{1,0:T(2,128)S(1)} %reshape.217, s32[1024]{0:T(1024)S(1)} %bitcast.90), kind=kCustom, calls=%fused_computation | custom fusion | bytes 16384 | tf_op jit(solution)/shard_map/jit(take_along_axis)/gather | solution.py:116
  226.9 7.3 %psum.14 = f32[2,512]{1,0:T(2,128)S(1)} all-reduce(f32[2,512]{1,0:T(2,128)S(1)} %and_select_fusion.1), channel_id=1, replica_groups=mesh['frame'=32,'row'=4] {'row'}, use_global_device_ids=true, to_apply=%region_11.12 | all-reduce | flops 1024 | bytes 8192 | tf_op jit(solution)/shard_map/psum | solution.py:119
  234.2 0.6 abs_reduce_fusion
  234.8 65.1 %psum.15 = f32[]{:T(128)} all-reduce(f32[]{:T(128)} %abs_reduce_fusion), channel_id=1, replica_groups=mesh['frame'=32,'row'=4] {'frame'}, use_global_device_ids=true, to_apply=%region_13.14 | all-reduce | flops 1 | bytes 8 | tf_op jit(solution)/shard_map/psum | solution.py:120
  (56 shorter events, 0.7 us)
Async XLA Ops:
  7.2 163.5 %copy-start = (bf16[1024,1024]{1,0:T(8,128)(2,1)S(1)}, bf16[1024,1024]{1,0:T(8,128)(2,1)}, u32[]{:S(2)}) copy-start(bf16[1024,1024]{1,0:T(8,128)(2,1)} %param.18) | copy-start | bytes 6291460
  7.2 3.4 %copy-start.2 = (bf16[2,256,1024]{2,1,0:T(8,128)(2,1)S(1)}, bf16[2,256,1024]{2,1,0:T(8,128)(2,1)}, u32[]{:S(2)}) copy-start(bf16[2,256,1024]{2,1,0:T(8,128)(2,1)} %param.15) | copy-start | bytes 3145732
  7.2 96.7 %all-gather.2.cloned.1.call-start = ((), (), s32[]{:S(2)}) async-start(), calls=%async_computation.2 | async-start | bytes 10485760 | tf_op jit(solution)/shard_map/all_gather | solution.py:47
  10.9 6.3 %copy-start.3 = (bf16[512,1024]{1,0:T(8,128)(2,1)}, bf16[512,1024]{1,0:T(8,128)(2,1)S(1)}, u32[]{:S(2)}) copy-start(bf16[512,1024]{1,0:T(8,128)(2,1)S(1)} %fusion.12) | copy-start | bytes 3145732
  21.4 4.1 %copy-start.12 = (bf16[6,256]{1,0:T(8,128)(2,1)S(1)}, bf16[6,256]{1,0:T(8,128)(2,1)}, u32[]{:S(2)}) copy-start(bf16[6,256]{1,0:T(8,128)(2,1)} %param.21) | copy-start | bytes 9220
  21.4 4.1 %copy-start.16 = (s32[64]{0:T(128)S(1)}, s32[64]{0:T(128)}, u32[]{:S(2)}) copy-start(s32[64]{0:T(128)} %param.22) | copy-start | bytes 772
  172.1 1.0 copy-start.4
  172.1 1.2 copy-start.6
  174.5 18.9 %copy-start.7 = (bf16[256,512]{1,0:T(8,128)(2,1)S(1)}, bf16[256,512]{1,0:T(8,128)(2,1)}, u32[]{:S(2)}) copy-start(bf16[256,512]{1,0:T(8,128)(2,1)} %param.24) | copy-start | bytes 786436
  174.5 16.9 %all-to-all-start = ((bf16[2,32,8,256]{3,2,0,1:T(8,128)(2,1)}), bf16[2,32,8,256]{3,2,0,1:T(8,128)(2,1)S(1)}, u32[]{:S(2)}, u32[]{:S(2)}) async-start(bf16[2,32,8,256]{3,2,0,1:T(8,128)(2,1)} %fusion.31), calls=%async_computation | async-start | bytes 524288 | tf_op jit(solution)/shard_map/all_to_all | solution.py:80
  193.2 2.7 copy-start.8
  196.6 3.0 copy-start.5
  200.9 3.4 %copy-start.9 = (bf16[256,256]{1,0:T(8,128)(2,1)S(1)}, bf16[256,256]{1,0:T(8,128)(2,1)}, u32[]{:S(2)}) copy-start(bf16[256,256]{1,0:T(8,128)(2,1)} %param.25) | copy-start | bytes 393220
  200.9 3.4 %copy-start.15 = (f32[256]{0:T(256)S(1)}, f32[256]{0:T(256)}, u32[]{:S(2)}) copy-start(f32[256]{0:T(256)} %param.26) | copy-start | bytes 3076
  200.9 9.3 %copy-start.11 = (s32[2,512]{1,0:T(2,128)S(1)}, s32[2,512]{1,0:T(2,128)}, u32[]{:S(2)}) copy-start(s32[2,512]{1,0:T(2,128)} %param.27) | copy-start | bytes 12292
  206.5 11.1 %all-to-all-start.1 = ((f32[64,1,8]{2,1,0:T(1,128)}), f32[64,1,8]{2,1,0:T(1,128)S(1)}, u32[]{:S(2)}, u32[]{:S(2)}) async-start(f32[64,1,8]{2,1,0:T(1,128)} %copy.83), calls=%async_computation.1 | async-start | bytes 65536 | tf_op jit(solution)/shard_map/all_to_all | solution.py:109
  217.7 9.2 %copy-start.1 = (f32[2,256]{1,0:T(2,128)}, f32[2,256]{1,0:T(2,128)S(1)}, u32[]{:S(2)}) copy-start(f32[2,256]{1,0:T(2,128)S(1)} %reshape.217) | copy-start | bytes 6148
  217.7 9.2 %copy-start.13 = (f32[2,512]{1,0:T(2,128)S(1)}, f32[2,512]{1,0:T(2,128)}, u32[]{:S(2)}) copy-start(f32[2,512]{1,0:T(2,128)} %param.28) | copy-start | bytes 12292
  217.7 9.2 %copy-start.14 = (s32[2,512]{1,0:T(2,128)S(1)}, s32[2,512]{1,0:T(2,128)}, u32[]{:S(2)}) copy-start(s32[2,512]{1,0:T(2,128)} %param.29) | copy-start | bytes 12292
  234.2 66.3 %copy-start.10 = (f32[2,512]{1,0:T(2,128)}, f32[2,512]{1,0:T(2,128)S(1)}, u32[]{:S(2)}) copy-start(f32[2,512]{1,0:T(2,128)S(1)} %psum.14) | copy-start | bytes 12292
Sparse Core Ops, SparseCore 0:
  17.3 86.5 all-gather.1
where the time goes:
time: 309 us; the launch traced here: 308 us
  waiting for transfers between devices  92 us (30%)
  blocking collectives  72.3 us (23%)
  matrix products  52.4 us (17%)
  local copies, waits for them, and re-layouts  43.1 us (14%)
  other arithmetic  20.8 us (7%)
  between operations  16.2 us (5%)
  starting transfers between devices  11.6 us (4%)
    all_gather x1, waiting for transfers between devices, body(): piece = lax.all_gather(keyval, 'row', axis=1, tiled=True)  75.6 us
    psum x1, blocking collectives, body(): abs_total = lax.psum(jnp.sum(jnp.abs(point_error)), 'frame')  65.1 us
    dot_general x1, matrix products, body(): jnp.einsum('fhqk,fkhd->fhqd', probs.astype(jnp.bfloat16), values, preferr...  16 us
    dot_general x1, matrix products, body(): jnp.einsum('fqhd,fkhd->fhqk', query, keys, preferred_element_type=jnp.flo...  15.6 us
    reduce_sum x1, other arithmetic, body(): total = jnp.sum(probs, axis=-1)  14.2 us
    slice x2, local copies, waits for them, and re-layouts, body(): keys = piece[:, :, :width].reshape(frames_dev, count, HEADS, head_dim)  12.1 us
    gather x2, local copies, waits for them, and re-layouts, body(): predicted = jnp.take_along_axis(depth_local, safe_index, axis=1)  9.12 us
    all_to_all x1, waiting for transfers between devices, body(): lax.all_to_all(feat, 'frame', split_axis=1, concat_axis=0, tiled=True)[:, 0]  8.98 us
  transfers between devices with their start and end apart: 3, of which 3 were waited for; matrix products, arithmetic and copies ran while one was open for 4% of the time, Pallas kernels for 0%

commit v1 on v0

v1 whole, which is shorter than its diff:
```python
import functools
import math

import jax
import jax.numpy as jnp
from jax import lax
from jax.experimental import pallas as pl
from jax.experimental.pallas import tpu as pltpu
from jax.sharding import PartitionSpec as P

MESH = pl.DeviceIdType.MESH
BF = jnp.bfloat16
F32 = jnp.float32
LOG2E = 1.4426950408889634
T_HEADS = 8
CAMERAS = 6
NT = (((1,), (1,)), ((), ()))


def normalize(values):
    mean = jnp.mean(values, axis=-1, keepdims=True)
    centred = values - mean
    var = jnp.mean(centred * centred, axis=-1, keepdims=True)
    return centred * lax.rsqrt(var + 1e-06)


def dot(a, b):
    return jnp.dot(a, b, preferred_element_type=F32)


def lanes(shape):
    return lax.broadcasted_iota(jnp.int32, shape, len(shape) - 1)


def rows(shape):
    return lax.broadcasted_iota(jnp.int32, shape, len(shape) - 2)


def kernel(
    x_ref, wq_h, wkv_h, wo_h, pin_h, patt_h, cam_ref, cid_ref, tq_h, tkv_h, tout_h, dread_ref,
    lpix_ref, ldep_ref, lval_ref,
    depth_ref, perr_ref, loss_ref,
    hid, wq, wkv, wo, pin, patt, tqw, tkvw, toutw,
    normed, qm, kbuf, vbuf, sbuf0, sbuf1, attn, featin, fsend, frecv,
    perm, spread, tattn, lsend, lall, dsend, drecv, dfull,
    wsem, hid_s, hid_r, kv_s, kv_r, lid_s, lid_r, feat_s, feat_r, dep_s, dep_r,
):
    f = lax.axis_index("frame")
    z = lax.axis_index("row")
    j = f // 2
    c = f % 2
    t = 4 * j + z

    barrier = pltpu.get_barrier_semaphore()

    @pl.loop(0, 128)
    def _(i):
        @pl.when(i != 4 * f + z)
        def _():
            pl.semaphore_signal(
                barrier, inc=1, device_id=(i // 4, i % 4), device_id_type=MESH
            )

    weights = [
        pltpu.make_async_copy(src, dst, wsem.at[k])
        for k, (src, dst) in enumerate(
            [(wkv_h, wkv), (wq_h, wq), (pin_h, pin), (wo_h, wo), (patt_h, patt),
             (tq_h, tqw), (tkv_h, tkvw), (tout_h, toutw)]
        )
    ]
    for copy in weights:
        copy.start()

    for k in range(4):
        part = slice(128 * k, 128 * k + 128)
        pixel = jnp.where(lval_ref[:, part] != 0, lpix_ref[:, part], -1).astype(F32)
        lsend[2 * k : 2 * k + 2, :] = pixel
        lsend[8 + 2 * k : 10 + 2 * k, :] = jnp.log(ldep_ref[:, part])
    own_points = pltpu.make_async_copy(lsend, lall.at[f], lid_r)
    own_points.start()

    pl.semaphore_wait(barrier, 127)

    def piece_copy(i, h):
        return pltpu.make_async_remote_copy(
            src_ref=x_ref.at[i, pl.ds(128 * h, 128)],
            dst_ref=hid.at[z],
            send_sem=hid_s.at[2 * i + h],
            recv_sem=hid_r.at[z],
            device_id=(2 * j + h, 2 * c + i),
            device_id_type=MESH,
        )

    def piece_here(i, h):
        return (2 * c + i == z) & (h == c)

    pieces = [(i, h) for i in range(2) for h in range(2)]
    for i, h in pieces:

        @pl.when(jnp.logical_not(piece_here(i, h)))
        def _():
            piece_copy(i, h).start()

        @pl.when(piece_here(i, h))
        def _():
            pltpu.make_async_copy(
                x_ref.at[i, pl.ds(128 * h, 128)], hid.at[z], hid_r.at[z]
            ).start()

    def points_copy(ff):
        return pltpu.make_async_remote_copy(
            src_ref=lsend,
            dst_ref=lall.at[f],
            send_sem=lid_s,
            recv_sem=lid_r,
            device_id=(ff, z),
            device_id_type=MESH,
        )

    @pl.loop(0, 32)
    def _(ff):
        @pl.when(ff != f)
        def _():
            points_copy(ff).start()

    row = rows((512, 512))
    perm[...] = jnp.where(lanes((512, 512)) == (row % 64) * 8 + row // 64, 1.0, 0.0).astype(BF)
    row = rows((256, 64))
    spread[...] = jnp.where(lanes((256, 64)) == 2 * (row // 8) + row % 2, 1.0, 0.0)

    def swap(buf, piece, k):
        return pltpu.make_async_remote_copy(
            src_ref=buf.at[pl.ds(128 * piece, 128)],
            dst_ref=buf.at[pl.ds(512 + 128 * piece, 128)],
            send_sem=kv_s.at[k, piece],
            recv_sem=kv_r.at[k, piece],
            device_id=(2 * j + 1 - c, z),
            device_id_type=MESH,
        )

    low = lanes((128, 1024)) % 128 < 64
    for copy in weights[:3]:
        copy.wait()

    @pl.loop(0, 4)
    def _(step):
        far = jnp.where(step == 2, 3, jnp.where(step == 3, 2, step))
        piece = (z + far) % 4
        pltpu.make_async_copy(hid.at[piece], hid.at[piece], hid_r.at[piece]).wait()
        n = normalize(hid[piece].astype(F32)).astype(BF)
        at = pl.ds(pl.multiple_of(128 * piece, 128), 128)
        normed[at, :] = n
        kbuf[at, :] = dot(normed[at, :], wkv[:, :1024]).astype(BF)
        swap(kbuf, piece, 0).start()
        vbuf[at, :] = dot(normed[at, :], wkv[:, 1024:]).astype(BF)
        swap(vbuf, piece, 1).start()
        q = dot(normed[at, :], wq[...]) * (LOG2E / 8.0)
        qm[0, at, :] = jnp.where(low, q, 0.0).astype(BF)
        qm[1, at, :] = jnp.where(low, 0.0, q).astype(BF)
        featin[at, :] = dot(normed[at, :], pin[...])

    camera = cid_ref[t]
    cam_row = jnp.zeros((1, 256), F32)
    for k in range(CAMERAS):
        cam_row = cam_row + cam_ref[k : k + 1, :].astype(F32) * jnp.where(camera == k, 1.0, 0.0)

    for piece in range(4):
        for k, buf in ((0, kbuf), (1, vbuf)):
            swap(buf, piece, k).wait_recv()
    for copy in weights[3:]:
        copy.wait()

    def scores(index, out):
        qc, pair = index // 8, index % 8
        at = pl.ds(pl.multiple_of(256 * qc, 256), 256)
        col = pl.ds(pl.multiple_of(128 * pair, 128), 128)
        q2 = qm[:, at, col].reshape(512, 128)
        out[...] = lax.dot_general(q2, kbuf[:, col], NT, preferred_element_type=F32)

    left = lanes((256, 128)) < 64
    ones = jnp.ones((1024, 128), BF)

    def attend(index, s_ref):
        qc, pair = index // 8, index % 8
        at = pl.ds(pl.multiple_of(256 * qc, 256), 256)
        col = pl.ds(pl.multiple_of(128 * pair, 128), 128)
        s = s_ref[...]
        p = jnp.exp2((s - jnp.max(s, axis=-1, keepdims=True)).astype(BF))
        o = dot(p, jnp.concatenate([vbuf[:, col], ones], axis=1))
        num = jnp.where(left, o[:256, :128], o[256:, :128])
        den = jnp.where(left, o[:256, 128:], o[256:, 128:])
        attn[at, col] = (num / den).astype(BF)

    def feat_copy(m):
        return pltpu.make_async_remote_copy(
            src_ref=fsend.at[m],
            dst_ref=frecv.at[t],
            send_sem=feat_s,
            recv_sem=feat_r,
            device_id=(2 * (m % 16) + c, m // 16),
            device_id_type=MESH,
        )

    mine = 16 * z + j
    scores(0, sbuf0)
    for qc in range(2):

        @pl.loop(0, 4)
        def _(step):
            index = 8 * qc + 2 * step
            scores(index + 1, sbuf1)
            attend(index, sbuf0)
            scores((index + 2) % 16, sbuf0)
            attend(index + 1, sbuf1)

        at = slice(256 * qc, 256 * qc + 256)
        own = hid[2 * qc : 2 * qc + 2].reshape(256, 1024).astype(F32)
        mixed = own + dot(attn[at, :], wo[...])
        after = normalize(mixed).astype(BF)
        feat = featin[at, :] + dot(after, patt[...]) + cam_row
        both = jnp.concatenate(
            [feat[:, :128].reshape(32, 8, 128), feat[:, 128:].reshape(32, 8, 128)], axis=1
        )
        fsend[32 * qc : 32 * qc + 32] = both.astype(BF)

        @pl.loop(32 * qc, 32 * qc + 32)
        def _(m):
            @pl.when(m != mine)
            def _():
                feat_copy(m).start()

            @pl.when(m == mine)
            def _():
                pltpu.make_async_copy(fsend.at[m], frecv.at[t], feat_r).start()

    pltpu.make_async_copy(frecv, frecv, feat_r).wait()

    got = frecv[...].astype(F32)
    got = jnp.concatenate(
        [got[:, :8, :].reshape(512, 128), got[:, 8:, :].reshape(512, 128)], axis=1
    ).astype(BF)
    feat = dot(perm[...], got)
    y = normalize(feat).astype(BF)
    tq = dot(y, tqw[...]) * (LOG2E / math.sqrt(32.0))
    tkv = dot(y, tkvw[...]).astype(BF)
    same = rows((512, 128)) // 64 % 2 == lanes((512, 128)) // 64
    head = lanes((128, 128)) // 32
    ones_t = jnp.ones((128, 128), BF)
    for b in range(4):
        for g in range(2):
            at = slice(128 * b, 128 * b + 128)
            col = slice(128 * g, 128 * g + 128)
            qb = tq[at, col]
            q4 = jnp.concatenate(
                [jnp.where(head == h, qb, 0.0).astype(BF) for h in range(4)], axis=0
            )
            s = lax.dot_general(q4, tkv[at, col], NT, preferred_element_type=F32)
            s = jnp.where(same, s, -jnp.inf)
            p = jnp.exp2(s - jnp.max(s, axis=-1, keepdims=True)).astype(BF)
            v = tkv[at, 256 + 128 * g : 384 + 128 * g]
            o = dot(p, jnp.concatenate([v, ones_t], axis=1))
            num = o[:128, :128]
            den = o[:128, 128:]
            for h in range(1, 4):
                num = jnp.where(head == h, o[128 * h : 128 * h + 128, :128], num)
                den = jnp.where(head == h, o[128 * h : 128 * h + 128, 128:], den)
            tattn[at, col] = (num / den).astype(BF)
    latent = feat + dot(tattn[...], toutw[...])
    logit = jnp.sum(latent * dread_ref[...], axis=-1, keepdims=True)

    lane = lanes((64, 128))
    block = jnp.zeros((64, 128), F32)
    for p in range(8):
        block = jnp.where(lane == 8 * j + p, logit[64 * p : 64 * p + 64, :], block)
    depth = 0.1 + jnp.maximum(block, 0.0) + jnp.log(1.0 + jnp.exp(-jnp.abs(block)))
    log_depth = jnp.dot(
        spread[...], jnp.log(depth), precision=lax.Precision.HIGHEST, preferred_element_type=F32
    )

    pltpu.make_async_copy(lall, lall, lid_r).wait()
    pixel = lall[:, :8, :].reshape(256, 128).astype(jnp.int32) - (256 * z + 128 * c)
    hit = (pixel >= 8 * j) & (pixel < 8 * j + 8)
    predicted = jnp.take_along_axis(log_depth, jnp.clip(pixel, 0, 127), axis=1)
    error = jnp.abs(predicted - lall[:, 8:, :].reshape(256, 128))
    partial = jnp.sum(jnp.where(hit, error, 0.0))

    mixed_out = jnp.where(lane // 8 == j, depth, partial)
    for k in range(64):
        dsend[k] = mixed_out[k : k + 1, :]

    slot = 2 * (16 * (2 * z + c) + j)

    def depth_copy(ff, zz):
        return pltpu.make_async_remote_copy(
            src_ref=dsend.at[pl.ds(2 * ff, 2)],
            dst_ref=drecv.at[pl.ds(slot, 2)],
            send_sem=dep_s,
            recv_sem=dep_r,
            device_id=(ff, zz),
            device_id_type=MESH,
        )

    @pl.loop(0, 128)
    def _(d):
        @pl.when(d != 4 * f + z)
        def _():
            depth_copy(d // 4, d % 4).start()

        @pl.when(d == 4 * f + z)
        def _():
            pltpu.make_async_copy(
                dsend.at[pl.ds(2 * f, 2)], drecv.at[pl.ds(slot, 2)], dep_r
            ).start()

    pltpu.make_async_copy(drecv, drecv, dep_r).wait()

    group = lanes((1, 128)) // 8
    total = jnp.zeros((1, 128), F32)
    for b in range(8):
        acc = [jnp.zeros((1, 128), F32) for _ in range(2)]
        for jj in range(16):
            for i in range(2):
                part = drecv[2 * (16 * b + jj) + i]
                acc[i] = jnp.where(group == jj, part, acc[i])
                if i == 0:
                    total = total + jnp.where(group == (jj + 1) % 16, part, 0.0)
        for i in range(2):
            dfull[2 * b + i] = acc[i]
    for h in range(2):
        for i in range(2):
            depth_ref[i : i + 1, 128 * h : 128 * h + 128] = dfull[2 * (2 * z + h) + i]
    loss_ref[...] = jnp.sum(total, axis=-1, keepdims=True) * (1.0 / (8 * 64 * 512))

    pixel = lsend[:8, :].astype(jnp.int32)
    odd = rows((8, 128)) % 2 == 1
    found = jnp.ones((8, 128), F32)
    for b in range(8):
        table = jnp.where(
            odd,
            jnp.broadcast_to(dfull[2 * b + 1], (8, 128)),
            jnp.broadcast_to(dfull[2 * b], (8, 128)),
        )
        local = pixel - 128 * b
        value = jnp.take_along_axis(table, jnp.clip(local, 0, 127), axis=1)
        found = jnp.where((local >= 0) & (local < 128), value, found)
    error = jnp.where(pixel >= 0, jnp.log(found) - lsend[8:, :], 0.0)
    for k in range(4):
        perr_ref[:, 128 * k : 128 * k + 128] = error[2 * k : 2 * k + 2, :]

    for i, h in pieces:

        @pl.when(jnp.logical_not(piece_here(i, h)))
        def _():
            piece_copy(i, h).wait_send()

    for piece in range(4):
        for k, buf in ((0, kbuf), (1, vbuf)):
            swap(buf, piece, k).wait_send()
    pltpu.make_async_copy(lall.at[pl.ds(0, 31)], lall.at[pl.ds(0, 31)], lid_s).wait()
    pltpu.make_async_copy(frecv.at[pl.ds(0, 63)], frecv.at[pl.ds(0, 63)], feat_s).wait()
    pltpu.make_async_copy(drecv.at[pl.ds(0, 254)], drecv.at[pl.ds(0, 254)], dep_s).wait()


def body(
    hidden_in, query_weight, kv_weight, out_weight, proj_in, proj_attn, camera_table, camera_id,
    t_query, t_kv, t_out, depth_read, lidar_pixel, lidar_depth, lidar_valid,
):
    hbm = pl.BlockSpec(memory_space=pl.ANY)
    vmem = pl.BlockSpec(memory_space=pltpu.VMEM)
    smem = pl.BlockSpec(memory_space=pltpu.SMEM)
    dma = pltpu.SemaphoreType.DMA
    depth_map, point_error, loss = pl.pallas_call(
        kernel,
        out_shape=(
            jax.ShapeDtypeStruct((2, 256), F32),
            jax.ShapeDtypeStruct((2, 512), F32),
            jax.ShapeDtypeStruct((1, 1), F32),
        ),
        in_specs=[
            hbm, hbm, hbm, hbm, hbm, hbm, vmem, smem, hbm, hbm, hbm, vmem, vmem, vmem, vmem,
        ],
        out_specs=(vmem, vmem, vmem),
        scratch_shapes=[
            pltpu.VMEM((4, 128, 1024), BF),
            pltpu.VMEM((1024, 1024), BF),
            pltpu.VMEM((1024, 2048), BF),
            pltpu.VMEM((1024, 1024), BF),
            pltpu.VMEM((1024, 256), BF),
            pltpu.VMEM((1024, 256), BF),
            pltpu.VMEM((256, 256), BF),
            pltpu.VMEM((256, 512), BF),
            pltpu.VMEM((256, 256), BF),
            pltpu.VMEM((512, 1024), BF),
            pltpu.VMEM((2, 512, 1024), BF),
            pltpu.VMEM((1024, 1024), BF),
            pltpu.VMEM((1024, 1024), BF),
            pltpu.VMEM((512, 1024), F32),
            pltpu.VMEM((512, 1024), F32),
            pltpu.VMEM((512, 1024), BF),
            pltpu.VMEM((512, 256), F32),
            pltpu.VMEM((64, 16, 128), BF),
            pltpu.VMEM((64, 16, 128), BF),
            pltpu.VMEM((512, 512), BF),
            pltpu.VMEM((256, 64), F32),
            pltpu.VMEM((512, 256), BF),
            pltpu.VMEM((16, 128), F32),
            pltpu.VMEM((32, 16, 128), F32),
            pltpu.VMEM((64, 1, 128), F32),
            pltpu.VMEM((256, 1, 128), F32),
            pltpu.VMEM((16, 1, 128), F32),
            dma((8,)), dma((4,)), dma((4,)), dma((2, 4)), dma((2, 4)),
            dma, dma, dma, dma, dma, dma,
        ],
        compiler_params=pltpu.CompilerParams(
            collective_id=0, has_side_effects=True, vmem_limit_bytes=56 * 2**20
        ),
        cost_estimate=pl.CostEstimate(
            flops=8_000_000_000, bytes_accessed=12_000_000, transcendentals=9_000_000
        ),
    )(
        hidden_in, query_weight, kv_weight, out_weight, proj_in, proj_attn, camera_table,
        camera_id, t_query, t_kv, t_out, depth_read.reshape(1, -1), lidar_pixel, lidar_depth,
        lidar_valid,
    )
    return depth_map, point_error, loss.reshape(())


def solution(mesh):
    return jax.shard_map(
        body,
        mesh=mesh,
        in_specs=(
            P("frame", "row", None),
            P(),
            P(),
            P(),
            P(),
            P(),
            P(),
            P(),
            P(),
            P(),
            P(),
            P(),
            P("frame", None),
            P("frame", None),
            P("frame", None),
        ),
        out_specs=(P("frame", "row"), P("frame", None), P()),
        check_vma=False,
    )
```

time: 309 us -> 69.4 us (0.22)
  waiting for transfers between devices: 92 us -> 0 us
  blocking collectives: 72.3 us -> 0 us
  Pallas kernels: 0 us -> 63.8 us
  matrix products: 52.4 us -> 0 us
  local copies, waits for them, and re-layouts: 43.1 us -> 2.5 us
  other arithmetic: 20.8 us -> 0 us
  between operations: 16.2 us -> 2.41 us
  starting transfers between devices: 11.6 us -> 0 us
    all_gather x1 -> x0, waiting for transfers between devices: 75.6 us -> none  [body(): piece = lax.all_gather(keyval, 'row', axis=1, tiled=True)]
    psum x2 -> x0, blocking collectives: 72.3 us -> none  [the longest x1 65.1 us: body(): abs_total = lax.psum(jnp.sum(jnp.abs(point_error)), 'frame')]
    pallas_call x0 -> x1, Pallas kernels: none -> 63.8 us  [body(): pl.pallas_call(kernel, out_shape=(jax.ShapeDtypeStruct((2, 256), F32), ja...]
    dot_general x13 -> x0, matrix products: 52.4 us -> none  [the longest x1 16 us: body(): jnp.einsum('fhqk,fkhd->fhqd', probs.astype(jnp.bfloat16), values, preferr...]
    slice x6 -> x0, local copies, waits for them, and re-layouts: 20.5 us -> none  [the longest x2 12.1 us: body(): keys = piece[:, :, :width].reshape(frames_dev, count, HEADS, head_dim)]
    reduce_sum x8 -> x0, other arithmetic: 19.4 us -> none  [the longest x1 14.2 us: body(): total = jnp.sum(probs, axis=-1)]
    all_to_all x2 -> x0, waiting for transfers between devices: 16.3 us -> none  [the longest x1 8.98 us: body(): lax.all_to_all(feat, 'frame', split_axis=1, concat_axis=0, tiled=True)[:, 0]]
    all_to_all x2 -> x0, starting transfers between devices: 11.6 us -> none  [the longest x1 7.9 us: body(): lax.all_to_all(feat, 'frame', split_axis=1, concat_axis=0, tiled=True)[:, 0]]
  transfers between devices with their start and end apart: 3 -> 0, of which waited for: 3 -> 0; matrix products, arithmetic and copies ran while one was open for 4% -> 0% of each run, Pallas kernels for 0% -> 0%
where the time goes in v1:
time: 69.4 us; the launch traced here: 68.7 us
  Pallas kernels  63.8 us (92%)
  local copies, waits for them, and re-layouts  2.5 us (4%)
  between operations  2.41 us (3%)
    pallas_call x1, Pallas kernels, body(): pl.pallas_call(kernel, out_shape=(jax.ShapeDtypeStruct((2, 256), F32), ja...  63.8 us
    unnamed x2, local copies, waits for them, and re-layouts  2.5 us

profile of v1, /device:TPU:1, one launch (start us, length us, event | category | flops | bytes accessed | tf_op | source)
XLA Modules:
  0.0 68.7 jit_solution(2999458498551452499)
XLA Ops:
  0.6 63.8 %shard_map.166 = (f32[2,256]{1,0:T(2,128)}, f32[2,512]{1,0:T(2,128)}, f32[1,1]{1,0:T(1,128)}) custom-call(bf16[2,256,1024]{2,1,0:T(8,128)(2,1)} %x_ref.1, bf16[1024,1024]{1,0:T(8,128)(2,1)} %wq_h.1, bf16[1024,2048]{1,0:T(8,128)(2,1)} %wkv_h.1, bf16[1024,1024]{1,0:T(8,128)(2,1)} %wo_h.1, bf16[1024,256]{1,0:T(8,128)(2,1)} %pin_h.1, bf16[1024,256]{1,0:T(8,128)(2,1)} %patt_h.1, ...), custom_call_target="tpu_custom_call" | custom-call | flops 8000000000 | bytes 12000000 | tf_op jit(solution)/shard_map/pallas_call | solution.py:372
  64.4 1.2 %copy.21 = f32[2,256]{1,0:T(2,128)} copy(f32[2,256]{1,0:T(2,128)} %get-tuple-element.12) | data formatting | bytes 4096
  65.6 1.3 %copy.22 = f32[2,512]{1,0:T(2,128)} copy(f32[2,512]{1,0:T(2,128)} %get-tuple-element.13) | data formatting | bytes 8192

commit v2 on v1

--- a/solution.py
+++ b/solution.py
@@ -43,7 +43,7 @@
     hid, wq, wkv, wo, pin, patt, tqw, tkvw, toutw,
     normed, qm, kbuf, vbuf, sbuf0, sbuf1, attn, featin, fsend, frecv,
     perm, spread, tattn, lsend, lall, dsend, drecv, dfull,
-    wsem, hid_s, hid_r, kv_s, kv_r, lid_s, lid_r, feat_s, feat_r, dep_s, dep_r,
+    here_x, here_y, wsem, hid_s, hid_r, kv_s, kv_r, lid_s, lid_r, feat_s, feat_r, dep_s, dep_r,
 ):
     f = lax.axis_index("frame")
     z = lax.axis_index("row")
@@ -53,13 +53,12 @@
 
     barrier = pltpu.get_barrier_semaphore()
 
-    @pl.loop(0, 128)
-    def _(i):
-        @pl.when(i != 4 * f + z)
-        def _():
-            pl.semaphore_signal(
-                barrier, inc=1, device_id=(i // 4, i % 4), device_id_type=MESH
-            )
+    gx, gy = f // 8, j % 4
+    column = [(2 * j + (c + dc) % 2, (z + dz) % 4) for dz in range(4) for dc in range(2)][1:]
+    along_x = [(8 * ((gx + d) % 4) + 2 * gy + c, z) for d in range(1, 4)]
+    along_y = [(8 * gx + 2 * ((gy + d) % 4) + c, z) for d in range(1, 4)]
+    for device in column + along_x + along_y:
+        pl.semaphore_signal(barrier, inc=1, device_id=device, device_id_type=MESH)
 
     weights = [
         pltpu.make_async_copy(src, dst, wsem.at[k])
@@ -79,7 +78,7 @@
     own_points = pltpu.make_async_copy(lsend, lall.at[f], lid_r)
     own_points.start()
 
-    pl.semaphore_wait(barrier, 127)
+    pl.semaphore_wait(barrier, 13)
 
     def piece_copy(i, h):
         return pltpu.make_async_remote_copy(
@@ -95,17 +94,46 @@
         return (2 * c + i == z) & (h == c)
 
     pieces = [(i, h) for i in range(2) for h in range(2)]
+    for far in (False, True):
+        for i, h in pieces:
+
+            @pl.when(jnp.logical_not(piece_here(i, h)) & (((2 * c + i - z + 4) % 4 == 2) == far))
+            def _():
+                piece_copy(i, h).start()
+
     for i, h in pieces:
-
-        @pl.when(jnp.logical_not(piece_here(i, h)))
-        def _():
-            piece_copy(i, h).start()
 
         @pl.when(piece_here(i, h))
         def _():
             pltpu.make_async_copy(
                 x_ref.at[i, pl.ds(128 * h, 128)], hid.at[z], hid_r.at[z]
             ).start()
+
+    for device in along_x:
+        pl.semaphore_signal(here_x, inc=1, device_id=device, device_id_type=MESH)
+
+    row = rows((512, 512))
+    perm[...] = jnp.where(lanes((512, 512)) == (row % 64) * 8 + row // 64, 1.0, 0.0).astype(BF)
+    row = rows((256, 64))
+    spread[...] = jnp.where(lanes((256, 64)) == 2 * (row // 8) + row % 2, 1.0, 0.0)
+
+    pl.semaphore_wait(here_x, 3)
+    for device in along_y:
+        pl.semaphore_signal(here_y, inc=1, device_id=device, device_id_type=MESH)
+
+    def swap(buf, piece, k):
+        return pltpu.make_async_remote_copy(
+            src_ref=buf.at[pl.ds(128 * piece, 128)],
+            dst_ref=buf.at[pl.ds(512 + 128 * piece, 128)],
+            send_sem=kv_s.at[k, piece],
+            recv_sem=kv_r.at[k, piece],
+            device_id=(2 * j + 1 - c, z),
+            device_id_type=MESH,
+        )
+
+    low = lanes((128, 1024)) % 128 < 64
+    for copy in weights[:3]:
+        copy.wait()
 
     def points_copy(ff):
         return pltpu.make_async_remote_copy(
@@ -117,35 +145,7 @@
             device_id_type=MESH,
         )
 
-    @pl.loop(0, 32)
-    def _(ff):
-        @pl.when(ff != f)
-        def _():
-            points_copy(ff).start()
-
-    row = rows((512, 512))
-    perm[...] = jnp.where(lanes((512, 512)) == (row % 64) * 8 + row // 64, 1.0, 0.0).astype(BF)
-    row = rows((256, 64))
-    spread[...] = jnp.where(lanes((256, 64)) == 2 * (row // 8) + row % 2, 1.0, 0.0)
-
-    def swap(buf, piece, k):
-        return pltpu.make_async_remote_copy(
-            src_ref=buf.at[pl.ds(128 * piece, 128)],
-            dst_ref=buf.at[pl.ds(512 + 128 * piece, 128)],
-            send_sem=kv_s.at[k, piece],
-            recv_sem=kv_r.at[k, piece],
-            device_id=(2 * j + 1 - c, z),
-            device_id_type=MESH,
-        )
-
-    low = lanes((128, 1024)) % 128 < 64
-    for copy in weights[:3]:
-        copy.wait()
-
-    @pl.loop(0, 4)
-    def _(step):
-        far = jnp.where(step == 2, 3, jnp.where(step == 3, 2, step))
-        piece = (z + far) % 4
+    def project(piece):
         pltpu.make_async_copy(hid.at[piece], hid.at[piece], hid_r.at[piece]).wait()
         n = normalize(hid[piece].astype(F32)).astype(BF)
         at = pl.ds(pl.multiple_of(128 * piece, 128), 128)
@@ -159,6 +159,21 @@
         qm[1, at, :] = jnp.where(low, 0.0, q).astype(BF)
         featin[at, :] = dot(normed[at, :], pin[...])
 
+    @pl.loop(0, 4)
+    def _(step):
+        far = jnp.where(step == 2, 3, jnp.where(step == 3, 2, step))
+        project((z + far) % 4)
+
+        @pl.when(step == 0)
+        def _():
+            pl.semaphore_wait(here_y, 3)
+
+            @pl.loop(0, 32)
+            def _(ff):
+                @pl.when(ff != f)
+                def _():
+                    points_copy(ff).start()
+
     camera = cid_ref[t]
     cam_row = jnp.zeros((1, 256), F32)
     for k in range(CAMERAS):
@@ -197,11 +212,12 @@
             dst_ref=frecv.at[t],
             send_sem=feat_s,
             recv_sem=feat_r,
-            device_id=(2 * (m % 16) + c, m // 16),
+            device_id=(2 * (m % 16) + c, (m // 16 + 2) % 4),
             device_id_type=MESH,
         )
 
-    mine = 16 * z + j
+    block_row = (z + 2) % 4
+    mine = 16 * block_row + j
     scores(0, sbuf0)
     for qc in range(2):
 
@@ -278,7 +294,7 @@
     )
 
     pltpu.make_async_copy(lall, lall, lid_r).wait()
-    pixel = lall[:, :8, :].reshape(256, 128).astype(jnp.int32) - (256 * z + 128 * c)
+    pixel = lall[:, :8, :].reshape(256, 128).astype(jnp.int32) - (256 * block_row + 128 * c)
     hit = (pixel >= 8 * j) & (pixel < 8 * j + 8)
     predicted = jnp.take_along_axis(log_depth, jnp.clip(pixel, 0, 127), axis=1)
     error = jnp.abs(predicted - lall[:, 8:, :].reshape(256, 128))
@@ -288,7 +304,7 @@
     for k in range(64):
         dsend[k] = mixed_out[k : k + 1, :]
 
-    slot = 2 * (16 * (2 * z + c) + j)
+    slot = 2 * (16 * (2 * block_row + c) + j)
 
     def depth_copy(ff, zz):
         return pltpu.make_async_remote_copy(
@@ -359,6 +375,12 @@
     pltpu.make_async_copy(lall.at[pl.ds(0, 31)], lall.at[pl.ds(0, 31)], lid_s).wait()
     pltpu.make_async_copy(frecv.at[pl.ds(0, 63)], frecv.at[pl.ds(0, 63)], feat_s).wait()
     pltpu.make_async_copy(drecv.at[pl.ds(0, 254)], drecv.at[pl.ds(0, 254)], dep_s).wait()
+
+
+def pass_on(depth_in, perr_in, loss_in, depth_out, perr_out, loss_out):
+    depth_out[...] = depth_in[...]
+    perr_out[...] = perr_in[...]
+    loss_out[...] = loss_in[...]
 
 
 def body(
@@ -408,6 +430,7 @@
             pltpu.VMEM((64, 1, 128), F32),
             pltpu.VMEM((256, 1, 128), F32),
             pltpu.VMEM((16, 1, 128), F32),
+            pltpu.SemaphoreType.REGULAR, pltpu.SemaphoreType.REGULAR,
             dma((8,)), dma((4,)), dma((4,)), dma((2, 4)), dma((2, 4)),
             dma, dma, dma, dma, dma, dma,
         ],
@@ -422,6 +445,16 @@
         camera_id, t_query, t_kv, t_out, depth_read.reshape(1, -1), lidar_pixel, lidar_depth,
         lidar_valid,
     )
+    depth_map, point_error, loss = pl.pallas_call(
+        pass_on,
+        out_shape=(
+            jax.ShapeDtypeStruct((2, 256), F32),
+            jax.ShapeDtypeStruct((2, 512), F32),
+            jax.ShapeDtypeStruct((1, 1), F32),
+        ),
+        in_specs=[vmem, vmem, vmem],
+        out_specs=(vmem, vmem, vmem),
+    )(depth_map, point_error, loss)
     return depth_map, point_error, loss.reshape(())
 
 

time: 69.4 us -> 62 us (0.89)
  Pallas kernels: 63.8 us -> 60.6 us
  local copies, waits for them, and re-layouts: 2.5 us -> 0 us
  between operations: 2.41 us -> 0.64 us
    pallas_call x1, Pallas kernels: 63.8 us -> 58.7 us  [body(): pl.pallas_call(kernel, out_shape=(jax.ShapeDtypeStruct((2, 256), F32), ja...]
    unnamed x2 -> x0, local copies, waits for them, and re-layouts: 2.5 us -> none
    pallas_call x0 -> x1, Pallas kernels: none -> 1.88 us  [body(): pl.pallas_call(pass_on, out_shape=(jax.ShapeDtypeStruct((2, 256), F32), j...]
where the time goes in v2:
time: 62 us; the launch traced here: 61.3 us
  Pallas kernels  60.6 us (98%)
  between operations  0.64 us (1%)
    pallas_call x1, Pallas kernels, body(): pl.pallas_call(kernel, out_shape=(jax.ShapeDtypeStruct((2, 256), F32), ja...  58.7 us
    pallas_call x1, Pallas kernels, body(): pl.pallas_call(pass_on, out_shape=(jax.ShapeDtypeStruct((2, 256), F32), j...  1.88 us

profile of v2, /device:TPU:1, one launch (start us, length us, event | category | flops | bytes accessed | tf_op | source)
XLA Modules:
  0.0 61.3 jit_solution(3682628983430138576)
XLA Ops:
  0.6 58.7 %shard_map.166 = (f32[2,256]{1,0:T(2,128)}, f32[2,512]{1,0:T(2,128)}, f32[1,1]{1,0:T(1,128)}) custom-call(bf16[2,256,1024]{2,1,0:T(8,128)(2,1)} %x_ref.1, bf16[1024,1024]{1,0:T(8,128)(2,1)} %wq_h.1, bf16[1024,2048]{1,0:T(8,128)(2,1)} %wkv_h.1, bf16[1024,1024]{1,0:T(8,128)(2,1)} %wo_h.1, bf16[1024,256]{1,0:T(8,128)(2,1)} %pin_h.1, bf16[1024,256]{1,0:T(8,128)(2,1)} %patt_h.1, ...), custom_call_target="tpu_custom_call" | custom-call | flops 8000000000 | bytes 12000000 | tf_op jit(solution)/shard_map/pallas_call | solution.py:394
  59.4 1.9 %shard_map.167 = (f32[2,256]{1,0:T(2,128)}, f32[2,512]{1,0:T(2,128)}, f32[1,1]{1,0:T(1,128)}) custom-call(f32[2,256]{1,0:T(2,128)} %get-tuple-element.9.depth_in, f32[2,512]{1,0:T(2,128)} %get-tuple-element.10.perr_in, f32[1,1]{1,0:T(1,128)} %get-tuple-element.11.loss_in), custom_call_target="tpu_custom_call" | custom-call | tf_op jit(solution)/shard_map/pallas_call | solution.py:448

commit v3 on v2

--- a/solution.py
+++ b/solution.py
@@ -41,7 +41,7 @@
     lpix_ref, ldep_ref, lval_ref,
     depth_ref, perr_ref, loss_ref,
     hid, wq, wkv, wo, pin, patt, tqw, tkvw, toutw,
-    normed, qm, kbuf, vbuf, sbuf0, sbuf1, attn, featin, fsend, frecv,
+    normed, qm, kbuf, vbuf, sbuf0, sbuf1, abuf0, abuf1, bbuf0, bbuf1, obuf, mbuf, attn, featin, fsend, frecv,
     perm, spread, tattn, lsend, lall, dsend, drecv, dfull,
     here_x, here_y, wsem, hid_s, hid_r, kv_s, kv_r, lid_s, lid_r, feat_s, feat_r, dep_s, dep_r,
 ):
@@ -80,12 +80,16 @@
 
     pl.semaphore_wait(barrier, 13)
 
+    def slot_of(i):
+        far = (z - 2 * c - i + 4) % 4
+        return jnp.where(far == 2, 3, jnp.where(far == 3, 2, far))
+
     def piece_copy(i, h):
         return pltpu.make_async_remote_copy(
             src_ref=x_ref.at[i, pl.ds(128 * h, 128)],
-            dst_ref=hid.at[z],
+            dst_ref=hid.at[slot_of(i)],
             send_sem=hid_s.at[2 * i + h],
-            recv_sem=hid_r.at[z],
+            recv_sem=hid_r.at[slot_of(i)],
             device_id=(2 * j + h, 2 * c + i),
             device_id_type=MESH,
         )
@@ -94,19 +98,22 @@
         return (2 * c + i == z) & (h == c)
 
     pieces = [(i, h) for i in range(2) for h in range(2)]
-    for far in (False, True):
-        for i, h in pieces:
-
-            @pl.when(jnp.logical_not(piece_here(i, h)) & (((2 * c + i - z + 4) % 4 == 2) == far))
-            def _():
-                piece_copy(i, h).start()
+
+    def is_far(i):
+        return (2 * c + i - z + 4) % 4 == 2
 
     for i, h in pieces:
 
+        @pl.when(jnp.logical_not(piece_here(i, h) | is_far(i)))
+        def _():
+            piece_copy(i, h).start()
+
+    for i, h in pieces:
+
         @pl.when(piece_here(i, h))
         def _():
             pltpu.make_async_copy(
-                x_ref.at[i, pl.ds(128 * h, 128)], hid.at[z], hid_r.at[z]
+                x_ref.at[i, pl.ds(128 * h, 128)], hid.at[0], hid_r.at[0]
             ).start()
 
     for device in along_x:
@@ -123,8 +130,8 @@
 
     def swap(buf, piece, k):
         return pltpu.make_async_remote_copy(
-            src_ref=buf.at[pl.ds(128 * piece, 128)],
-            dst_ref=buf.at[pl.ds(512 + 128 * piece, 128)],
+            src_ref=buf.at[pl.ds(256 * piece, 128)],
+            dst_ref=buf.at[pl.ds(256 * piece + 128, 128)],
             send_sem=kv_s.at[k, piece],
             recv_sem=kv_r.at[k, piece],
             device_id=(2 * j + 1 - c, z),
@@ -149,24 +156,35 @@
         pltpu.make_async_copy(hid.at[piece], hid.at[piece], hid_r.at[piece]).wait()
         n = normalize(hid[piece].astype(F32)).astype(BF)
         at = pl.ds(pl.multiple_of(128 * piece, 128), 128)
+        keys = pl.ds(pl.multiple_of(256 * piece, 256), 128)
         normed[at, :] = n
-        kbuf[at, :] = dot(normed[at, :], wkv[:, :1024]).astype(BF)
+        kbuf[keys, :] = dot(normed[at, :], wkv[:, :1024]).astype(BF)
         swap(kbuf, piece, 0).start()
-        vbuf[at, :] = dot(normed[at, :], wkv[:, 1024:]).astype(BF)
+        vbuf[keys, :] = dot(normed[at, :], wkv[:, 1024:]).astype(BF)
         swap(vbuf, piece, 1).start()
         q = dot(normed[at, :], wq[...]) * (LOG2E / 8.0)
         qm[0, at, :] = jnp.where(low, q, 0.0).astype(BF)
         qm[1, at, :] = jnp.where(low, 0.0, q).astype(BF)
         featin[at, :] = dot(normed[at, :], pin[...])
 
-    @pl.loop(0, 4)
+    @pl.loop(0, 3)
     def _(step):
-        far = jnp.where(step == 2, 3, jnp.where(step == 3, 2, step))
-        project((z + far) % 4)
+        project(step)
 
         @pl.when(step == 0)
         def _():
             pl.semaphore_wait(here_y, 3)
+            for i, h in pieces:
+
+                @pl.when(jnp.logical_not(piece_here(i, h) | is_far(i)))
+                def _():
+                    piece_copy(i, h).wait_send()
+
+            for i, h in pieces:
+
+                @pl.when(is_far(i))
+                def _():
+                    piece_copy(i, h).start()
 
             @pl.loop(0, 32)
             def _(ff):
@@ -179,32 +197,57 @@
     for k in range(CAMERAS):
         cam_row = cam_row + cam_ref[k : k + 1, :].astype(F32) * jnp.where(camera == k, 1.0, 0.0)
 
-    for piece in range(4):
+    for piece in range(3):
         for k, buf in ((0, kbuf), (1, vbuf)):
             swap(buf, piece, k).wait_recv()
     for copy in weights[3:]:
         copy.wait()
 
-    def scores(index, out):
-        qc, pair = index // 8, index % 8
-        at = pl.ds(pl.multiple_of(256 * qc, 256), 256)
+    def scores_first(pair, out):
         col = pl.ds(pl.multiple_of(128 * pair, 128), 128)
-        q2 = qm[:, at, col].reshape(512, 128)
-        out[...] = lax.dot_general(q2, kbuf[:, col], NT, preferred_element_type=F32)
-
-    left = lanes((256, 128)) < 64
-    ones = jnp.ones((1024, 128), BF)
-
-    def attend(index, s_ref):
-        qc, pair = index // 8, index % 8
-        at = pl.ds(pl.multiple_of(256 * qc, 256), 256)
+        q2 = qm[:, :384, col].reshape(768, 128)
+        out[...] = lax.dot_general(q2, kbuf[:768, col], NT, preferred_element_type=F32)
+
+    def values(at, col, count):
+        return jnp.concatenate([vbuf[at, col], jnp.ones((count, 128), BF)], axis=1)
+
+    def attend_first(pair, s_ref):
         col = pl.ds(pl.multiple_of(128 * pair, 128), 128)
         s = s_ref[...]
+        top = jnp.max(s, axis=-1, keepdims=True)
+        p = jnp.exp2((s - top).astype(BF))
+        obuf[pair] = dot(p, values(slice(0, 768), col, 768))
+        mbuf[pair] = jnp.broadcast_to(top, (768, 128))
+
+    def scores_last(pair, out_a, out_b):
+        col = pl.ds(pl.multiple_of(128 * pair, 128), 128)
+        q2 = qm[:, :384, col].reshape(768, 128)
+        out_a[...] = lax.dot_general(q2, kbuf[768:, col], NT, preferred_element_type=F32)
+        q2 = qm[:, 384:, col].reshape(256, 128)
+        out_b[...] = lax.dot_general(q2, kbuf[:, col], NT, preferred_element_type=F32)
+
+    def heads_of(o, count):
+        left = lanes((count, 128)) < 64
+        num = jnp.where(left, o[:count, :128], o[count:, :128])
+        den = jnp.where(left, o[:count, 128:], o[count:, 128:])
+        return (num / den).astype(BF)
+
+    def attend_last(pair, a_ref, b_ref):
+        col = pl.ds(pl.multiple_of(128 * pair, 128), 128)
+        s = a_ref[...]
+        before = mbuf[pair]
+        top = jnp.maximum(before, jnp.max(s, axis=-1, keepdims=True))
+        p = jnp.exp2((s - jnp.concatenate([top, top], axis=1)).astype(BF))
+        keep = jnp.exp2(before - top)
+        o = obuf[pair] * jnp.concatenate([keep, keep], axis=1)
+        o = o + dot(p, values(slice(768, 1024), col, 256))
+        attn[:384, col] = heads_of(o, 384)
+        s = b_ref[...]
         p = jnp.exp2((s - jnp.max(s, axis=-1, keepdims=True)).astype(BF))
-        o = dot(p, jnp.concatenate([vbuf[:, col], ones], axis=1))
-        num = jnp.where(left, o[:256, :128], o[256:, :128])
-        den = jnp.where(left, o[:256, 128:], o[256:, 128:])
-        attn[at, col] = (num / den).astype(BF)
+        attn[384:, col] = heads_of(dot(p, values(slice(0, 1024), col, 1024)), 128)
+
+    def row_of(piece):
+        return (z + 2 + jnp.where(piece == 2, 3, jnp.where(piece == 3, 2, piece))) % 4
 
     def feat_copy(m):
         return pltpu.make_async_remote_copy(
@@ -212,23 +255,39 @@
             dst_ref=frecv.at[t],
             send_sem=feat_s,
             recv_sem=feat_r,
-            device_id=(2 * (m % 16) + c, (m // 16 + 2) % 4),
+            device_id=(2 * (m % 16) + c, row_of(m // 16)),
             device_id_type=MESH,
         )
 
     block_row = (z + 2) % 4
-    mine = 16 * block_row + j
-    scores(0, sbuf0)
+    mine = 48 + j
+    scores_first(0, sbuf0)
+
+    @pl.loop(0, 4)
+    def _(step):
+        @pl.when(step == 3)
+        def _():
+            project(3)
+
+        pair = 2 * step
+        scores_first(pair + 1, sbuf1)
+        attend_first(pair, sbuf0)
+        scores_first((pair + 2) % 8, sbuf0)
+        attend_first(pair + 1, sbuf1)
+
+    for k, buf in ((0, kbuf), (1, vbuf)):
+        swap(buf, 3, k).wait_recv()
+    scores_last(0, abuf0, bbuf0)
+
+    @pl.loop(0, 4)
+    def _(step):
+        pair = 2 * step
+        scores_last(pair + 1, abuf1, bbuf1)
+        attend_last(pair, abuf0, bbuf0)
+        scores_last((pair + 2) % 8, abuf0, bbuf0)
+        attend_last(pair + 1, abuf1, bbuf1)
+
     for qc in range(2):
-
-        @pl.loop(0, 4)
-        def _(step):
-            index = 8 * qc + 2 * step
-            scores(index + 1, sbuf1)
-            attend(index, sbuf0)
-            scores((index + 2) % 16, sbuf0)
-            attend(index + 1, sbuf1)
-
         at = slice(256 * qc, 256 * qc + 256)
         own = hid[2 * qc : 2 * qc + 2].reshape(256, 1024).astype(F32)
         mixed = own + dot(attn[at, :], wo[...])
@@ -365,7 +424,7 @@
 
     for i, h in pieces:
 
-        @pl.when(jnp.logical_not(piece_here(i, h)))
+        @pl.when(is_far(i))
         def _():
             piece_copy(i, h).wait_send()
 
@@ -377,10 +436,13 @@
     pltpu.make_async_copy(drecv.at[pl.ds(0, 254)], drecv.at[pl.ds(0, 254)], dep_s).wait()
 
 
-def pass_on(depth_in, perr_in, loss_in, depth_out, perr_out, loss_out):
-    depth_out[...] = depth_in[...]
-    perr_out[...] = perr_in[...]
-    loss_out[...] = loss_in[...]
+def pass_on(depth_in, perr_in, loss_in, depth_out, perr_out, loss_out, sem):
+    pairs = [(depth_in, depth_out), (perr_in, perr_out), (loss_in, loss_out)]
+    copies = [pltpu.make_async_copy(a, b, sem.at[k]) for k, (a, b) in enumerate(pairs)]
+    for copy in copies:
+        copy.start()
+    for copy in copies:
+        copy.wait()
 
 
 def body(
@@ -416,8 +478,14 @@
             pltpu.VMEM((2, 512, 1024), BF),
             pltpu.VMEM((1024, 1024), BF),
             pltpu.VMEM((1024, 1024), BF),
-            pltpu.VMEM((512, 1024), F32),
-            pltpu.VMEM((512, 1024), F32),
+            pltpu.VMEM((768, 768), F32),
+            pltpu.VMEM((768, 768), F32),
+            pltpu.VMEM((768, 256), F32),
+            pltpu.VMEM((768, 256), F32),
+            pltpu.VMEM((256, 1024), F32),
+            pltpu.VMEM((256, 1024), F32),
+            pltpu.VMEM((8, 768, 256), F32),
+            pltpu.VMEM((8, 768, 128), F32),
             pltpu.VMEM((512, 1024), BF),
             pltpu.VMEM((512, 256), F32),
             pltpu.VMEM((64, 16, 128), BF),
@@ -452,8 +520,9 @@
             jax.ShapeDtypeStruct((2, 512), F32),
             jax.ShapeDtypeStruct((1, 1), F32),
         ),
-        in_specs=[vmem, vmem, vmem],
-        out_specs=(vmem, vmem, vmem),
+        in_specs=[hbm, hbm, hbm],
+        out_specs=(hbm, hbm, hbm),
+        scratch_shapes=[dma((3,))],
     )(depth_map, point_error, loss)
     return depth_map, point_error, loss.reshape(())
 

time: 62 us -> 57.5 us (0.927)
  Pallas kernels: 60.6 us -> 56.3 us
    pallas_call x1, Pallas kernels: 58.7 us -> 54.3 us  [body(): pl.pallas_call(kernel, out_shape=(jax.ShapeDtypeStruct((2, 256), F32), ja...]
where the time goes in v3:
time: 57.5 us; the launch traced here: 56.9 us
  Pallas kernels  56.3 us (98%)
  between operations  0.64 us (1%)
    pallas_call x1, Pallas kernels, body(): pl.pallas_call(kernel, out_shape=(jax.ShapeDtypeStruct((2, 256), F32), ja...  54.3 us
    pallas_call x1, Pallas kernels, body(): pl.pallas_call(pass_on, out_shape=(jax.ShapeDtypeStruct((2, 256), F32), j...  1.92 us

profile of v3, /device:TPU:1, one launch (start us, length us, event | category | flops | bytes accessed | tf_op | source)
XLA Modules:
  0.0 56.9 jit_solution(1747988622532624699)
XLA Ops:
  0.6 54.3 %shard_map.166 = (f32[2,256]{1,0:T(2,128)}, f32[2,512]{1,0:T(2,128)}, f32[1,1]{1,0:T(1,128)}) custom-call(bf16[2,256,1024]{2,1,0:T(8,128)(2,1)} %x_ref.1, bf16[1024,1024]{1,0:T(8,128)(2,1)} %wq_h.1, bf16[1024,2048]{1,0:T(8,128)(2,1)} %wkv_h.1, bf16[1024,1024]{1,0:T(8,128)(2,1)} %wo_h.1, bf16[1024,256]{1,0:T(8,128)(2,1)} %pin_h.1, bf16[1024,256]{1,0:T(8,128)(2,1)} %patt_h.1, ...), custom_call_target="tpu_custom_call" | custom-call | flops 8000000000 | bytes 12000000 | tf_op jit(solution)/shard_map/pallas_call | solution.py:456
  55.0 1.9 %shard_map.167 = (f32[2,256]{1,0:T(2,128)}, f32[2,512]{1,0:T(2,128)}, f32[1,1]{1,0:T(1,128)}) custom-call(f32[2,256]{1,0:T(2,128)} %get-tuple-element.9.depth_in, f32[2,512]{1,0:T(2,128)} %get-tuple-element.10.perr_in, f32[1,1]{1,0:T(1,128)} %get-tuple-element.11.loss_in), custom_call_target="tpu_custom_call" | custom-call | tf_op jit(solution)/shard_map/pallas_call | solution.py:516

commit v4 on v3

--- a/solution.py
+++ b/solution.py
@@ -41,7 +41,7 @@
     lpix_ref, ldep_ref, lval_ref,
     depth_ref, perr_ref, loss_ref,
     hid, wq, wkv, wo, pin, patt, tqw, tkvw, toutw,
-    normed, qm, kbuf, vbuf, sbuf0, sbuf1, abuf0, abuf1, bbuf0, bbuf1, obuf, mbuf, attn, featin, fsend, frecv,
+    normed, qm, ktbuf, vbuf, sbuf0, sbuf1, abuf0, abuf1, bbuf0, bbuf1, obuf, mbuf, attn, featin, fsend, frecv,
     perm, spread, tattn, lsend, lall, dsend, drecv, dfull,
     here_x, here_y, wsem, hid_s, hid_r, kv_s, kv_r, lid_s, lid_r, feat_s, feat_r, dep_s, dep_r,
 ):
@@ -128,17 +128,26 @@
     for device in along_y:
         pl.semaphore_signal(here_y, inc=1, device_id=device, device_id_type=MESH)
 
-    def swap(buf, piece, k):
+    def swap_keys(piece):
         return pltpu.make_async_remote_copy(
-            src_ref=buf.at[pl.ds(256 * piece, 128)],
-            dst_ref=buf.at[pl.ds(256 * piece + 128, 128)],
-            send_sem=kv_s.at[k, piece],
-            recv_sem=kv_r.at[k, piece],
+            src_ref=ktbuf.at[2 * piece],
+            dst_ref=ktbuf.at[2 * piece + 1],
+            send_sem=kv_s.at[0, piece],
+            recv_sem=kv_r.at[0, piece],
             device_id=(2 * j + 1 - c, z),
             device_id_type=MESH,
         )
 
-    low = lanes((128, 1024)) % 128 < 64
+    def swap_values(piece):
+        return pltpu.make_async_remote_copy(
+            src_ref=vbuf.at[pl.ds(256 * piece, 128)],
+            dst_ref=vbuf.at[pl.ds(256 * piece + 128, 128)],
+            send_sem=kv_s.at[1, piece],
+            recv_sem=kv_r.at[1, piece],
+            device_id=(2 * j + 1 - c, z),
+            device_id_type=MESH,
+        )
+
     for copy in weights[:3]:
         copy.wait()
 
@@ -152,45 +161,48 @@
             device_id_type=MESH,
         )
 
-    def project(piece):
-        pltpu.make_async_copy(hid.at[piece], hid.at[piece], hid_r.at[piece]).wait()
-        n = normalize(hid[piece].astype(F32)).astype(BF)
-        at = pl.ds(pl.multiple_of(128 * piece, 128), 128)
-        keys = pl.ds(pl.multiple_of(256 * piece, 256), 128)
-        normed[at, :] = n
-        kbuf[keys, :] = dot(normed[at, :], wkv[:, :1024]).astype(BF)
-        swap(kbuf, piece, 0).start()
-        vbuf[keys, :] = dot(normed[at, :], wkv[:, 1024:]).astype(BF)
-        swap(vbuf, piece, 1).start()
+    def project(first, count):
+        for piece in range(first, first + count):
+            pltpu.make_async_copy(hid.at[piece], hid.at[piece], hid_r.at[piece]).wait()
+        size = 128 * count
+        at = slice(128 * first, 128 * first + size)
+        own = hid[first : first + count].reshape(size, 1024)
+        normed[at, :] = normalize(own.astype(F32)).astype(BF)
+        key = dot(normed[at, :], wkv[:, :1024]).astype(BF)
+        for k in range(count):
+            ktbuf[2 * (first + k)] = key[128 * k : 128 * k + 128].T
+            swap_keys(first + k).start()
+        value = dot(normed[at, :], wkv[:, 1024:]).astype(BF)
+        for k in range(count):
+            row = 256 * (first + k)
+            vbuf[row : row + 128, :] = value[128 * k : 128 * k + 128]
+            swap_values(first + k).start()
         q = dot(normed[at, :], wq[...]) * (LOG2E / 8.0)
+        low = lanes((size, 1024)) % 128 < 64
         qm[0, at, :] = jnp.where(low, q, 0.0).astype(BF)
         qm[1, at, :] = jnp.where(low, 0.0, q).astype(BF)
         featin[at, :] = dot(normed[at, :], pin[...])
 
-    @pl.loop(0, 3)
-    def _(step):
-        project(step)
-
-        @pl.when(step == 0)
+    project(0, 1)
+    pl.semaphore_wait(here_y, 3)
+
+    @pl.loop(1, 32)
+    def _(ff):
+        points_copy((f + ff) % 32).start()
+
+    for i, h in pieces:
+
+        @pl.when(jnp.logical_not(piece_here(i, h) | is_far(i)))
         def _():
-            pl.semaphore_wait(here_y, 3)
-            for i, h in pieces:
-
-                @pl.when(jnp.logical_not(piece_here(i, h) | is_far(i)))
-                def _():
-                    piece_copy(i, h).wait_send()
-
-            for i, h in pieces:
-
-                @pl.when(is_far(i))
-                def _():
-                    piece_copy(i, h).start()
-
-            @pl.loop(0, 32)
-            def _(ff):
-                @pl.when(ff != f)
-                def _():
-                    points_copy(ff).start()
+            piece_copy(i, h).wait_send()
+
+    for i, h in pieces:
+
+        @pl.when(is_far(i))
+        def _():
+            piece_copy(i, h).start()
+
+    project(1, 2)
 
     camera = cid_ref[t]
     cam_row = jnp.zeros((1, 256), F32)
@@ -198,15 +210,18 @@
         cam_row = cam_row + cam_ref[k : k + 1, :].astype(F32) * jnp.where(camera == k, 1.0, 0.0)
 
     for piece in range(3):
-        for k, buf in ((0, kbuf), (1, vbuf)):
-            swap(buf, piece, k).wait_recv()
+        swap_keys(piece).wait_recv()
+        swap_values(piece).wait_recv()
     for copy in weights[3:]:
         copy.wait()
+
+    def keys_of(first, last, col):
+        return jnp.concatenate([ktbuf[k, col, :] for k in range(first, last)], axis=1)
 
     def scores_first(pair, out):
         col = pl.ds(pl.multiple_of(128 * pair, 128), 128)
         q2 = qm[:, :384, col].reshape(768, 128)
-        out[...] = lax.dot_general(q2, kbuf[:768, col], NT, preferred_element_type=F32)
+        out[...] = dot(q2, keys_of(0, 6, col))
 
     def values(at, col, count):
         return jnp.concatenate([vbuf[at, col], jnp.ones((count, 128), BF)], axis=1)
@@ -222,9 +237,9 @@
     def scores_last(pair, out_a, out_b):
         col = pl.ds(pl.multiple_of(128 * pair, 128), 128)
         q2 = qm[:, :384, col].reshape(768, 128)
-        out_a[...] = lax.dot_general(q2, kbuf[768:, col], NT, preferred_element_type=F32)
+        out_a[...] = dot(q2, keys_of(6, 8, col))
         q2 = qm[:, 384:, col].reshape(256, 128)
-        out_b[...] = lax.dot_general(q2, kbuf[:, col], NT, preferred_element_type=F32)
+        out_b[...] = dot(q2, keys_of(0, 8, col))
 
     def heads_of(o, count):
         left = lanes((count, 128)) < 64
@@ -247,27 +262,30 @@
         attn[384:, col] = heads_of(dot(p, values(slice(0, 1024), col, 1024)), 128)
 
     def row_of(piece):
-        return (z + 2 + jnp.where(piece == 2, 3, jnp.where(piece == 3, 2, piece))) % 4
-
-    def feat_copy(m):
+        return (z + 2 + (0, 1, 3, 2)[piece]) % 4
+
+    offsets = [(dx, dy) for dx in range(4) for dy in range(4)]
+    offsets.sort(key=lambda o: min(o[0], 4 - o[0]) + min(o[1], 4 - o[1]))
+
+    def feat_copy(piece, dx, dy):
+        other = 4 * ((gx + dx) % 4) + (gy + dy) % 4
         return pltpu.make_async_remote_copy(
-            src_ref=fsend.at[m],
+            src_ref=fsend.at[16 * piece + other],
             dst_ref=frecv.at[t],
             send_sem=feat_s,
             recv_sem=feat_r,
-            device_id=(2 * (m % 16) + c, row_of(m // 16)),
+            device_id=(2 * other + c, row_of(piece)),
             device_id_type=MESH,
         )
 
     block_row = (z + 2) % 4
-    mine = 48 + j
     scores_first(0, sbuf0)
 
     @pl.loop(0, 4)
     def _(step):
         @pl.when(step == 3)
         def _():
-            project(3)
+            project(3, 1)
 
         pair = 2 * step
         scores_first(pair + 1, sbuf1)
@@ -275,8 +293,8 @@
         scores_first((pair + 2) % 8, sbuf0)
         attend_first(pair + 1, sbuf1)
 
-    for k, buf in ((0, kbuf), (1, vbuf)):
-        swap(buf, 3, k).wait_recv()
+    swap_keys(3).wait_recv()
+    swap_values(3).wait_recv()
     scores_last(0, abuf0, bbuf0)
 
     @pl.loop(0, 4)
@@ -287,26 +305,18 @@
         scores_last((pair + 2) % 8, abuf0, bbuf0)
         attend_last(pair + 1, abuf1, bbuf1)
 
-    for qc in range(2):
-        at = slice(256 * qc, 256 * qc + 256)
-        own = hid[2 * qc : 2 * qc + 2].reshape(256, 1024).astype(F32)
-        mixed = own + dot(attn[at, :], wo[...])
+    for piece in range(4):
+        at = slice(128 * piece, 128 * piece + 128)
+        mixed = hid[piece].astype(F32) + dot(attn[at, :], wo[...])
         after = normalize(mixed).astype(BF)
         feat = featin[at, :] + dot(after, patt[...]) + cam_row
         both = jnp.concatenate(
-            [feat[:, :128].reshape(32, 8, 128), feat[:, 128:].reshape(32, 8, 128)], axis=1
-        )
-        fsend[32 * qc : 32 * qc + 32] = both.astype(BF)
-
-        @pl.loop(32 * qc, 32 * qc + 32)
-        def _(m):
-            @pl.when(m != mine)
-            def _():
-                feat_copy(m).start()
-
-            @pl.when(m == mine)
-            def _():
-                pltpu.make_async_copy(fsend.at[m], frecv.at[t], feat_r).start()
+            [feat[:, :128].reshape(16, 8, 128), feat[:, 128:].reshape(16, 8, 128)], axis=1
+        )
+        fsend[16 * piece : 16 * piece + 16] = both.astype(BF)
+        for dx, dy in reversed(offsets[int(piece == 3) :]):
+            feat_copy(piece, dx, dy).start()
+    pltpu.make_async_copy(fsend.at[48 + j], frecv.at[t], feat_r).start()
 
     pltpu.make_async_copy(frecv, frecv, feat_r).wait()
 
@@ -375,17 +385,18 @@
             device_id_type=MESH,
         )
 
-    @pl.loop(0, 128)
-    def _(d):
-        @pl.when(d != 4 * f + z)
-        def _():
-            depth_copy(d // 4, d % 4).start()
-
-        @pl.when(d == 4 * f + z)
-        def _():
-            pltpu.make_async_copy(
-                dsend.at[pl.ds(2 * f, 2)], drecv.at[pl.ds(slot, 2)], dep_r
-            ).start()
+    def hops(offset):
+        return sum(min(d, 4 - d) for d in offset[:3])
+
+    everyone = [
+        (dx, dy, dz, dc)
+        for dx in range(4) for dy in range(4) for dz in range(4) for dc in range(2)
+    ][1:]
+    for dx, dy, dz, dc in sorted(everyone, key=hops, reverse=True):
+        depth_copy(
+            8 * ((gx + dx) % 4) + 2 * ((gy + dy) % 4) + (c + dc) % 2, (z + dz) % 4
+        ).start()
+    pltpu.make_async_copy(dsend.at[pl.ds(2 * f, 2)], drecv.at[pl.ds(slot, 2)], dep_r).start()
 
     pltpu.make_async_copy(drecv, drecv, dep_r).wait()
 
@@ -429,8 +440,8 @@
             piece_copy(i, h).wait_send()
 
     for piece in range(4):
-        for k, buf in ((0, kbuf), (1, vbuf)):
-            swap(buf, piece, k).wait_send()
+        swap_keys(piece).wait_send()
+        swap_values(piece).wait_send()
     pltpu.make_async_copy(lall.at[pl.ds(0, 31)], lall.at[pl.ds(0, 31)], lid_s).wait()
     pltpu.make_async_copy(frecv.at[pl.ds(0, 63)], frecv.at[pl.ds(0, 63)], feat_s).wait()
     pltpu.make_async_copy(drecv.at[pl.ds(0, 254)], drecv.at[pl.ds(0, 254)], dep_s).wait()
@@ -476,7 +487,7 @@
             pltpu.VMEM((256, 256), BF),
             pltpu.VMEM((512, 1024), BF),
             pltpu.VMEM((2, 512, 1024), BF),
-            pltpu.VMEM((1024, 1024), BF),
+            pltpu.VMEM((8, 1024, 128), BF),
             pltpu.VMEM((1024, 1024), BF),
             pltpu.VMEM((768, 768), F32),
             pltpu.VMEM((768, 768), F32),

time: 57.5 us -> 55.8 us (0.970)
  Pallas kernels: 56.3 us -> 54.8 us
    pallas_call x1, Pallas kernels: 54.3 us -> 52.9 us  [body(): pl.pallas_call(kernel, out_shape=(jax.ShapeDtypeStruct((2, 256), F32), ja...]
where the time goes in v4:
time: 55.8 us; the launch traced here: 55.6 us
  Pallas kernels  54.8 us (98%)
  between operations  0.81 us (1%)
    pallas_call x1, Pallas kernels, body(): pl.pallas_call(kernel, out_shape=(jax.ShapeDtypeStruct((2, 256), F32), ja...  52.9 us
    pallas_call x1, Pallas kernels, body(): pl.pallas_call(pass_on, out_shape=(jax.ShapeDtypeStruct((2, 256), F32), j...  1.92 us

profile of v4, /device:TPU:1, one launch (start us, length us, event | category | flops | bytes accessed | tf_op | source)
XLA Modules:
  0.0 55.6 jit_solution(3269472918867830400)
XLA Ops:
  0.6 52.9 %shard_map.166 = (f32[2,256]{1,0:T(2,128)}, f32[2,512]{1,0:T(2,128)}, f32[1,1]{1,0:T(1,128)}) custom-call(bf16[2,256,1024]{2,1,0:T(8,128)(2,1)} %x_ref.1, bf16[1024,1024]{1,0:T(8,128)(2,1)} %wq_h.1, bf16[1024,2048]{1,0:T(8,128)(2,1)} %wkv_h.1, bf16[1024,1024]{1,0:T(8,128)(2,1)} %wo_h.1, bf16[1024,256]{1,0:T(8,128)(2,1)} %pin_h.1, bf16[1024,256]{1,0:T(8,128)(2,1)} %patt_h.1, ...), custom_call_target="tpu_custom_call" | custom-call | flops 8000000000 | bytes 12000000 | tf_op jit(solution)/shard_map/pallas_call | solution.py:467
  53.5 1.9 %shard_map.167 = (f32[2,256]{1,0:T(2,128)}, f32[2,512]{1,0:T(2,128)}, f32[1,1]{1,0:T(1,128)}) custom-call(f32[2,256]{1,0:T(2,128)} %get-tuple-element.9.depth_in, f32[2,512]{1,0:T(2,128)} %get-tuple-element.10.perr_in, f32[1,1]{1,0:T(1,128)} %get-tuple-element.11.loss_in), custom_call_target="tpu_custom_call" | custom-call | tf_op jit(solution)/shard_map/pallas_call | solution.py:527

commit v5 on v4

--- a/solution.py
+++ b/solution.py
@@ -215,11 +215,14 @@
     for copy in weights[3:]:
         copy.wait()
 
+    def at_pair(pair):
+        return pl.ds(128 * pair if isinstance(pair, int) else pl.multiple_of(128 * pair, 128), 128)
+
     def keys_of(first, last, col):
         return jnp.concatenate([ktbuf[k, col, :] for k in range(first, last)], axis=1)
 
     def scores_first(pair, out):
-        col = pl.ds(pl.multiple_of(128 * pair, 128), 128)
+        col = at_pair(pair)
         q2 = qm[:, :384, col].reshape(768, 128)
         out[...] = dot(q2, keys_of(0, 6, col))
 
@@ -227,19 +230,22 @@
         return jnp.concatenate([vbuf[at, col], jnp.ones((count, 128), BF)], axis=1)
 
     def attend_first(pair, s_ref):
-        col = pl.ds(pl.multiple_of(128 * pair, 128), 128)
+        col = at_pair(pair)
         s = s_ref[...]
         top = jnp.max(s, axis=-1, keepdims=True)
         p = jnp.exp2((s - top).astype(BF))
         obuf[pair] = dot(p, values(slice(0, 768), col, 768))
         mbuf[pair] = jnp.broadcast_to(top, (768, 128))
 
-    def scores_last(pair, out_a, out_b):
-        col = pl.ds(pl.multiple_of(128 * pair, 128), 128)
+    def scores_merge(pair, out):
+        col = at_pair(pair)
         q2 = qm[:, :384, col].reshape(768, 128)
-        out_a[...] = dot(q2, keys_of(6, 8, col))
+        out[...] = dot(q2, keys_of(6, 8, col))
+
+    def scores_last(pair, out):
+        col = at_pair(pair)
         q2 = qm[:, 384:, col].reshape(256, 128)
-        out_b[...] = dot(q2, keys_of(0, 8, col))
+        out[...] = dot(q2, keys_of(0, 8, col))
 
     def heads_of(o, count):
         left = lanes((count, 128)) < 64
@@ -247,9 +253,9 @@
         den = jnp.where(left, o[:count, 128:], o[count:, 128:])
         return (num / den).astype(BF)
 
-    def attend_last(pair, a_ref, b_ref):
-        col = pl.ds(pl.multiple_of(128 * pair, 128), 128)
-        s = a_ref[...]
+    def attend_merge(pair, s_ref):
+        col = at_pair(pair)
+        s = s_ref[...]
         before = mbuf[pair]
         top = jnp.maximum(before, jnp.max(s, axis=-1, keepdims=True))
         p = jnp.exp2((s - jnp.concatenate([top, top], axis=1)).astype(BF))
@@ -257,7 +263,10 @@
         o = obuf[pair] * jnp.concatenate([keep, keep], axis=1)
         o = o + dot(p, values(slice(768, 1024), col, 256))
         attn[:384, col] = heads_of(o, 384)
-        s = b_ref[...]
+
+    def attend_last(pair, s_ref):
+        col = at_pair(pair)
+        s = s_ref[...]
         p = jnp.exp2((s - jnp.max(s, axis=-1, keepdims=True)).astype(BF))
         attn[384:, col] = heads_of(dot(p, values(slice(0, 1024), col, 1024)), 128)
 
@@ -280,42 +289,52 @@
 
     block_row = (z + 2) % 4
     scores_first(0, sbuf0)
-
-    @pl.loop(0, 4)
-    def _(step):
-        @pl.when(step == 3)
-        def _():
+    for pair in range(0, 8, 2):
+        if pair == 6:
             project(3, 1)
-
-        pair = 2 * step
         scores_first(pair + 1, sbuf1)
         attend_first(pair, sbuf0)
-        scores_first((pair + 2) % 8, sbuf0)
+        if pair < 6:
+            scores_first(pair + 2, sbuf0)
         attend_first(pair + 1, sbuf1)
 
     swap_keys(3).wait_recv()
     swap_values(3).wait_recv()
-    scores_last(0, abuf0, bbuf0)
-
-    @pl.loop(0, 4)
-    def _(step):
-        pair = 2 * step
-        scores_last(pair + 1, abuf1, bbuf1)
-        attend_last(pair, abuf0, bbuf0)
-        scores_last((pair + 2) % 8, abuf0, bbuf0)
-        attend_last(pair + 1, abuf1, bbuf1)
-
-    for piece in range(4):
-        at = slice(128 * piece, 128 * piece + 128)
-        mixed = hid[piece].astype(F32) + dot(attn[at, :], wo[...])
+    def send_features(first, count):
+        size = 128 * count
+        at = slice(128 * first, 128 * first + size)
+        own = hid[first : first + count].reshape(size, 1024).astype(F32)
+        mixed = own + dot(attn[at, :], wo[...])
         after = normalize(mixed).astype(BF)
         feat = featin[at, :] + dot(after, patt[...]) + cam_row
+        blocks = 16 * count
         both = jnp.concatenate(
-            [feat[:, :128].reshape(16, 8, 128), feat[:, 128:].reshape(16, 8, 128)], axis=1
-        )
-        fsend[16 * piece : 16 * piece + 16] = both.astype(BF)
-        for dx, dy in reversed(offsets[int(piece == 3) :]):
-            feat_copy(piece, dx, dy).start()
+            [feat[:, :128].reshape(blocks, 8, 128), feat[:, 128:].reshape(blocks, 8, 128)], axis=1
+        )
+        fsend[16 * first : 16 * first + blocks] = both.astype(BF)
+        for piece in range(first, first + count):
+            for dx, dy in reversed(offsets[int(piece == 3) :]):
+                feat_copy(piece, dx, dy).start()
+
+    scores_merge(0, abuf0)
+    for pair in range(0, 8, 2):
+        scores_merge(pair + 1, abuf1)
+        attend_merge(pair, abuf0)
+        if pair < 6:
+            scores_merge(pair + 2, abuf0)
+        else:
+            scores_last(0, bbuf0)
+        attend_merge(pair + 1, abuf1)
+
+    send_features(0, 3)
+    for pair in range(0, 8, 2):
+        scores_last(pair + 1, bbuf1)
+        attend_last(pair, bbuf0)
+        if pair < 6:
+            scores_last(pair + 2, bbuf0)
+        attend_last(pair + 1, bbuf1)
+
+    send_features(3, 1)
     pltpu.make_async_copy(fsend.at[48 + j], frecv.at[t], feat_r).start()
 
     pltpu.make_async_copy(frecv, frecv, feat_r).wait()

time: 55.8 us -> 53.2 us (0.953)
  Pallas kernels: 54.8 us -> 52.2 us
    pallas_call x1, Pallas kernels: 52.9 us -> 50.3 us  [body(): pl.pallas_call(kernel, out_shape=(jax.ShapeDtypeStruct((2, 256), F32), ja...]
where the time goes in v5:
time: 53.2 us; the launch traced here: 53.1 us
  Pallas kernels  52.2 us (98%)
  between operations  0.81 us (2%)
    pallas_call x1, Pallas kernels, body(): pl.pallas_call(kernel, out_shape=(jax.ShapeDtypeStruct((2, 256), F32), ja...  50.3 us
    pallas_call x1, Pallas kernels, body(): pl.pallas_call(pass_on, out_shape=(jax.ShapeDtypeStruct((2, 256), F32), j...  1.92 us

profile of v5, /device:TPU:1, one launch (start us, length us, event | category | flops | bytes accessed | tf_op | source)
XLA Modules:
  0.0 53.1 jit_solution(14087640687448421791)
XLA Ops:
  0.6 50.3 %shard_map.166 = (f32[2,256]{1,0:T(2,128)}, f32[2,512]{1,0:T(2,128)}, f32[1,1]{1,0:T(1,128)}) custom-call(bf16[2,256,1024]{2,1,0:T(8,128)(2,1)} %x_ref.1, bf16[1024,1024]{1,0:T(8,128)(2,1)} %wq_h.1, bf16[1024,2048]{1,0:T(8,128)(2,1)} %wkv_h.1, bf16[1024,1024]{1,0:T(8,128)(2,1)} %wo_h.1, bf16[1024,256]{1,0:T(8,128)(2,1)} %pin_h.1, bf16[1024,256]{1,0:T(8,128)(2,1)} %patt_h.1, ...), custom_call_target="tpu_custom_call" | custom-call | flops 8000000000 | bytes 12000000 | tf_op jit(solution)/shard_map/pallas_call | solution.py:486
  51.0 1.9 %shard_map.167 = (f32[2,256]{1,0:T(2,128)}, f32[2,512]{1,0:T(2,128)}, f32[1,1]{1,0:T(1,128)}) custom-call(f32[2,256]{1,0:T(2,128)} %get-tuple-element.9.depth_in, f32[2,512]{1,0:T(2,128)} %get-tuple-element.10.perr_in, f32[1,1]{1,0:T(1,128)} %get-tuple-element.11.loss_in), custom_call_target="tpu_custom_call" | custom-call | tf_op jit(solution)/shard_map/pallas_call | solution.py:546

commit v6 on v5

--- a/solution.py
+++ b/solution.py
@@ -211,9 +211,6 @@
 
     for piece in range(3):
         swap_keys(piece).wait_recv()
-        swap_values(piece).wait_recv()
-    for copy in weights[3:]:
-        copy.wait()
 
     def at_pair(pair):
         return pl.ds(128 * pair if isinstance(pair, int) else pl.multiple_of(128 * pair, 128), 128)
@@ -289,6 +286,8 @@
 
     block_row = (z + 2) % 4
     scores_first(0, sbuf0)
+    for piece in range(3):
+        swap_values(piece).wait_recv()
     for pair in range(0, 8, 2):
         if pair == 6:
             project(3, 1)
@@ -299,7 +298,6 @@
         attend_first(pair + 1, sbuf1)
 
     swap_keys(3).wait_recv()
-    swap_values(3).wait_recv()
     def send_features(first, count):
         size = 128 * count
         at = slice(128 * first, 128 * first + size)
@@ -317,6 +315,9 @@
                 feat_copy(piece, dx, dy).start()
 
     scores_merge(0, abuf0)
+    swap_values(3).wait_recv()
+    for copy in weights[3:]:
+        copy.wait()
     for pair in range(0, 8, 2):
         scores_merge(pair + 1, abuf1)
         attend_merge(pair, abuf0)

time: 53.2 us -> 52.9 us (level)
  no operation moved by 1% of the time
where the time goes in v6:
time: 52.9 us; the launch traced here: 52.8 us
  Pallas kernels  52 us (98%)
  between operations  0.81 us (2%)
    pallas_call x1, Pallas kernels, body(): pl.pallas_call(kernel, out_shape=(jax.ShapeDtypeStruct((2, 256), F32), ja...  50 us
    pallas_call x1, Pallas kernels, body(): pl.pallas_call(pass_on, out_shape=(jax.ShapeDtypeStruct((2, 256), F32), j...  1.92 us

profile of v6, /device:TPU:1, one launch (start us, length us, event | category | flops | bytes accessed | tf_op | source)
XLA Modules:
  0.0 52.8 jit_solution(13386746226640929748)
XLA Ops:
  0.6 50.0 %shard_map.166 = (f32[2,256]{1,0:T(2,128)}, f32[2,512]{1,0:T(2,128)}, f32[1,1]{1,0:T(1,128)}) custom-call(bf16[2,256,1024]{2,1,0:T(8,128)(2,1)} %x_ref.1, bf16[1024,1024]{1,0:T(8,128)(2,1)} %wq_h.1, bf16[1024,2048]{1,0:T(8,128)(2,1)} %wkv_h.1, bf16[1024,1024]{1,0:T(8,128)(2,1)} %wo_h.1, bf16[1024,256]{1,0:T(8,128)(2,1)} %pin_h.1, bf16[1024,256]{1,0:T(8,128)(2,1)} %patt_h.1, ...), custom_call_target="tpu_custom_call" | custom-call | flops 8000000000 | bytes 12000000 | tf_op jit(solution)/shard_map/pallas_call | solution.py:487
  50.7 1.9 %shard_map.167 = (f32[2,256]{1,0:T(2,128)}, f32[2,512]{1,0:T(2,128)}, f32[1,1]{1,0:T(1,128)}) custom-call(f32[2,256]{1,0:T(2,128)} %get-tuple-element.9.depth_in, f32[2,512]{1,0:T(2,128)} %get-tuple-element.10.perr_in, f32[1,1]{1,0:T(1,128)} %get-tuple-element.11.loss_in), custom_call_target="tpu_custom_call" | custom-call | tf_op jit(solution)/shard_map/pallas_call | solution.py:547
